TPU v7x, 256 devices: a whole 4x4x8 slice. The times are simulated.
256 devices in a mesh: section: 2 (over x_lo), dp: 8 (over z), tensor: 16 (over x_hi, y, core).
Axes of the slice: x: 4 (x_hi: 2, x_lo: 2; x = x_hi * 2 + x_lo), y: 4, z: 8, core: 2. Of those that a mesh axis runs over, the one named last changes fastest.
Arguments:
- grads: bfloat16 [2, 8192, 8192], P('section', 'dp', 'tensor')
- groups: int32 [2, 8192], P('section', 'tensor'), may hold values from 0 to 3
- acts: bfloat16 [2, 8192, 14336], P('section', 'dp', 'tensor'), may hold values from -6 to 6
Outputs:
- hessian: float32 [2, 14336, 3584], P('section', ('tensor', 'dp'))
All inputs are finite; a program needn't handle non-finite values.
Results may differ from a plain program's by a relative error of at most 0.0009.
Values may be sent and summed in bfloat16 or wider, within the bound.
No kernel may reach another device: no remote copies, remote signals or barrier semaphores. Data moves between devices by JAX's collectives and lax.ppermute only.
A program may use at most 256 MiB of HBM per device.

v0:
```python
import functools

import jax
import jax.numpy as jnp
from jax import lax
from jax.experimental import pallas as pl
from jax.experimental.pallas import tpu as pltpu
from jax.sharding import PartitionSpec as P

D = 8192
GROUPS = 4
DP = 8
LANES = 128
OWN = (0, 3, 4, 5)
SENT = jnp.float16
VMEM_LIMIT = 8 * 1024 * 1024
PRODUCT_VMEM_LIMIT = 24 * 1024 * 1024
KEPT = 576


def shift(value, axis, steps):
    count = lax.axis_size(axis)
    return lax.ppermute(value, axis, [(i, (i + steps) % count) for i in range(count)])


def split_kernel(groups_ref, own_ref, kept_ref, moved_ref):
    kept_ref[...] = own_ref[:KEPT]
    moved_ref[: own_ref.shape[0] - KEPT] = own_ref[KEPT:]
    names = groups_ref[...].astype(jnp.float32)
    moved_ref[own_ref.shape[0] - KEPT :] = jnp.broadcast_to(names, (16, names.shape[1])).astype(
        moved_ref.dtype
    )


def split(groups, own):
    tokens, channels = own.shape
    return pl.pallas_call(
        split_kernel,
        out_shape=[
            jax.ShapeDtypeStruct((KEPT, channels), own.dtype),
            jax.ShapeDtypeStruct((tokens - KEPT + 16, channels), own.dtype),
        ],
        compiler_params=pltpu.CompilerParams(vmem_limit_bytes=VMEM_LIMIT),
    )(groups, own)


def square_kernel(start, named, groups_ref, own_ref, *refs):
    count = refs[-1].shape[1]
    total = own_ref[start : start + count].astype(jnp.float32)
    groups = groups_ref[...]
    if len(refs) == 2:
        total = total + refs[0][:count].astype(jnp.float32)
        if named:
            groups = refs[0][count:].astype(jnp.float32).astype(jnp.int32)
    group = lax.broadcasted_iota(jnp.int32, (16, groups_ref.shape[1]), 0)
    onehot = jnp.where(groups == group, 1.0, 0.0).astype(jnp.bfloat16)
    rest = total * total
    result = jnp.zeros((16, count), jnp.float32)
    for _ in range(3):
        part = rest.astype(jnp.bfloat16)
        rest = rest - part.astype(jnp.float32)
        result += lax.dot_general(
            onehot, part, (((1,), (1,)), ((), ())), preferred_element_type=jnp.float32
        )
    refs[-1][...] = result[:GROUPS]


def group_squares(groups, own, start, stop, *other, named=False):
    return pl.pallas_call(
        functools.partial(square_kernel, start, named),
        out_shape=jax.ShapeDtypeStruct((GROUPS, stop - start), jnp.float32),
        compiler_params=pltpu.CompilerParams(vmem_limit_bytes=VMEM_LIMIT),
    )(groups, own, *other)


def section_weights(own, groups, meanwhile):
    tokens = own.shape[0]
    kept, moved = split(groups, own)
    first = lax.ppermute(moved, "section", [(0, 1)])
    later = lax.ppermute(kept, "section", [(1, 0)])
    alone = group_squares(groups, own, KEPT, tokens)
    first, alone, *meanwhile = lax.optimization_barrier((first, alone, *meanwhile))
    back = group_squares(groups, own, KEPT, tokens, first, named=True)
    back = lax.ppermute(back, "section", [(1, 0)])
    rest = jnp.where(lax.axis_index("section") == 0, back, alone)
    partial = jnp.concatenate([group_squares(groups, own, 0, KEPT, later), rest], 1)
    count = lax.axis_size("tensor")
    partial += lax.ppermute(partial, "tensor", [(i, i ^ 1) for i in range(count)])
    chips = [list(range(core, count, 2)) for core in (0, 1)]
    spread = jnp.broadcast_to(partial[None], (count // 2, GROUPS, tokens))
    spread = lax.all_to_all(spread, "tensor", 0, 0, axis_index_groups=chips, tiled=True)
    return spread.sum(0) / D, *meanwhile


def pair_tiles(mean, out_ref, at):
    count = mean.shape[0]
    whole = mean.shape[1] // LANES
    for c in range(whole):
        out_ref[at + c * count : at + (c + 1) * count] = mean[:, c * LANES : (c + 1) * LANES]
    rest = mean[:, whole * LANES :]
    at += whole * count
    out_ref[at : at + count // 2] = jnp.concatenate([rest[: count // 2], rest[count // 2 :]], 1)


def dot(left, right):
    return lax.dot_general(
        left, right, (((1,), (1,)), ((), ())), preferred_element_type=jnp.float32
    )


def mean_of_orders(one, two, scaled_one, scaled_two):
    count = one.shape[0]
    other = dot(jnp.concatenate(scaled_one, 0), two)
    other = [other[g * count : (g + 1) * count] for g in range(GROUPS)]
    return 0.5 * (dot(one, jnp.concatenate(scaled_two, 0)) + jnp.concatenate(other, 1))


def first_kernel(one, two, weight_ref, turned_ref, peak_ref, top_ref, out_ref):
    most = weight_ref[...] * (peak_ref[...] * peak_ref[...])
    most = jnp.max(jnp.max(most, axis=0, keepdims=True), axis=1, keepdims=True)
    most = jnp.ceil(jnp.log2(jnp.maximum(most, 1e-30)))
    top_ref[...] = jnp.broadcast_to(most, top_ref.shape)
    count = turned_ref.shape[0] // DP
    rows, scaled = [], []
    for b in (one, two):
        rows.append(turned_ref[b * count : (b + 1) * count])
        wide = rows[-1].astype(jnp.float32)
        scaled.append(
            [(wide * weight_ref[g : g + 1]).astype(jnp.bfloat16) for g in range(GROUPS)]
        )
    pair_tiles(mean_of_orders(*rows, *scaled), out_ref, 0)


def first_sums(weight, turned, peak, one, two, shape):
    return pl.pallas_call(
        functools.partial(first_kernel, one, two),
        out_shape=[
            jax.ShapeDtypeStruct((8, LANES), jnp.float32),
            jax.ShapeDtypeStruct((shape, LANES), jnp.float32),
        ],
        compiler_params=pltpu.CompilerParams(vmem_limit_bytes=PRODUCT_VMEM_LIMIT),
        cost_estimate=pl.CostEstimate(flops=1, bytes_accessed=1, transcendentals=0),
    )(weight, turned, peak)


def product_kernel(make, table_ref, factors_ref, turned_ref, *refs):
    out_ref = refs[-1]
    scaled_ref = refs[0] if make else factors_ref
    count = turned_ref.shape[0] // DP
    tiles = DP * count // LANES

    def place(b):
        return pl.ds(pl.multiple_of(lax.rem(b, DP) * count, 16), count)

    def scale(b, carry):
        rows = turned_ref[place(b)].astype(jnp.float32)
        for g in range(GROUPS):
            scaled_ref[g, place(b)] = (rows * factors_ref[g : g + 1]).astype(jnp.bfloat16)
        return carry

    def work(job, carry):
        block, half, one, two = (table_ref[job, n] for n in range(4))
        right = [scaled_ref[2 * half + q, place(block + c)] for q in (0, 1) for c in OWN]
        result = dot(turned_ref[place(block)], jnp.concatenate(right, 0))
        for c in range(tiles):
            out_ref[job, c * count : (c + 1) * count] = result[:, c * LANES : (c + 1) * LANES]
        mean = mean_of_orders(
            turned_ref[place(one)],
            turned_ref[place(two)],
            [scaled_ref[g, place(one)] for g in range(GROUPS)],
            [scaled_ref[g, place(two)] for g in range(GROUPS)],
        )
        pair_tiles(mean, out_ref.at[job], tiles * count)
        return carry

    if make:
        lax.fori_loop(0, DP, scale, 0)
    lax.fori_loop(0, out_ref.shape[0], work, 0, unroll=2)


def products(factors, turned, shape, jobs):
    make = factors.ndim == 2
    table = jnp.array([[b % DP, half, x % DP, y % DP] for b, half, x, y in jobs], jnp.int32)
    out_shape = [jax.ShapeDtypeStruct((len(jobs), shape, LANES), jnp.float32)]
    if make:
        out_shape.insert(0, jax.ShapeDtypeStruct((GROUPS, *turned.shape), jnp.bfloat16))
    vmem = pl.BlockSpec(memory_space=pltpu.VMEM)
    return pl.pallas_call(
        functools.partial(product_kernel, make),
        in_specs=[pl.BlockSpec(memory_space=pltpu.SMEM), vmem, vmem],
        out_specs=[vmem] * len(out_shape),
        out_shape=out_shape,
        compiler_params=pltpu.CompilerParams(vmem_limit_bytes=PRODUCT_VMEM_LIMIT),
        cost_estimate=pl.CostEstimate(flops=1, bytes_accessed=1, transcendentals=0),
    )(table, factors, turned)


def finish_kernel(factor, me_ref, *refs):
    *sums_refs, out_ref = refs
    own_refs, one_refs, two_refs, got_refs = (sums_refs[n : n + 2] for n in (0, 2, 4, 6))
    count = out_ref.shape[0]
    size = own_refs[0].shape[0]
    width = DP * count
    whole = GROUPS * count // LANES

    def pair(ref, got_ref, at):
        def rows(start, stop):
            return ref[start:stop] + got_ref[at + start : at + stop]

        parts = [rows(c * count, (c + 1) * count) for c in range(whole)]
        rest = rows(whole * count, whole * count + count // 2)
        rest = jnp.concatenate([rest[:, : LANES // 2], rest[:, LANES // 2 :]], 0)
        return jnp.concatenate([*parts, rest], 1)

    both = [(side, 1 - side) for side in (0, 1)]
    ones = [pair(one_refs[i], got_refs[j], size + one_refs[i].shape[0]) for i, j in both]
    twos = [pair(two_refs[i], got_refs[j], size) for i, j in both]
    for p in (0, 1):
        parts = []
        for at in range(0, size, count):
            parts.append(own_refs[p][at : at + count] + got_refs[p][at : at + count])
        own = jnp.concatenate(parts, 1)
        for q in (0, 1):
            g = 2 * p + q
            blocks = [None] * DP
            for n, c in enumerate(OWN):
                at = (q * len(OWN) + n) * count
                blocks[c] = own[:, at : at + count]
            group = slice(g * count, (g + 1) * count)
            blocks[1], blocks[2] = ones[0][:, group], twos[0][:, group]
            blocks[7], blocks[6] = ones[1][:, group].T, twos[1][:, group].T
            row = jnp.concatenate(blocks, 1)
            row = pltpu.roll(row, me_ref[0] * count, 1)
            out_ref[:, g * width : (g + 1) * width] = row * factor


def finish(me, own, ones, twos, got, count, factor):
    vmem = pl.BlockSpec(memory_space=pltpu.VMEM)
    return pl.pallas_call(
        functools.partial(finish_kernel, factor),
        in_specs=[pl.BlockSpec(memory_space=pltpu.SMEM)] + [vmem] * 8,
        out_specs=vmem,
        out_shape=jax.ShapeDtypeStruct((count, GROUPS * DP * count), jnp.float32),
        compiler_params=pltpu.CompilerParams(vmem_limit_bytes=PRODUCT_VMEM_LIMIT),
    )(me, *own, *ones, *twos, *got)


def on_device(grads, groups, acts):
    me = lax.axis_index("dp").astype(jnp.int32)
    cols = acts[0]
    tokens, width = cols.shape
    rows = width // DP
    turned = cols.T
    peak = jnp.max(jnp.abs(turned), axis=0, keepdims=True).astype(jnp.float32)
    turned = lax.dynamic_slice_in_dim(jnp.concatenate([turned, turned], 0), me * rows, width, 0)
    weight, turned, peak = section_weights(grads[0], groups, (turned, peak))

    size = width // LANES * rows
    pair = GROUPS * rows * rows // LANES
    long, short = size + pair + 8, pair + 8

    top, ahead0 = first_sums(weight, turned, peak, 3, 5, short)
    top = top[:1]
    way, both = (1, -1), (0, 1)
    scaled, begin = products(weight, turned, long, [(3, 1, 3, 4), (5, 0, 4, 5)])
    sums = {(2, 0): begin[0], (2, 1): begin[1]}
    bits = 15 - (tokens * DP - 1).bit_length()

    def pack(value, level):
        room = lax.broadcasted_iota(jnp.int32, value.shape, 0) >= value.shape[0] - 8
        return jnp.where(room, level, value * jnp.exp2(bits - level)).astype(SENT)

    def tag_of(value):
        return value[-1:].astype(jnp.float32)

    def unpack(value):
        return value.astype(jnp.float32) * jnp.exp2(tag_of(value) - bits)

    def send(packed):
        return [shift(packed[i], "dp", way[i]) for i in both]

    start = shift(pack(ahead0, top), "dp", 1)
    got, sent = {}, {}
    sent[2] = [pack(sums[2, i], top) for i in both]
    got[2] = send(sent[2])

    def later(*steps):
        nonlocal scaled
        scaled = lax.optimization_barrier((scaled, *(v for pair in sent.values() for v in pair)))[0]
        jobs = []
        for k in steps:
            ahead, behind, distance = (2 - k // 2, k // 2 - 4, 2) if k % 2 else (4 - k // 2, k // 2 - 5, 1)
            block = (8 - k) // 2 + k % 2
            for i, one in enumerate((ahead, behind)):
                half = i if k == 8 else (k + 1 + i) % 2
                jobs.append((block * way[i], half, one, one + distance))
        result = products(scaled, turned, long, jobs)[0]
        for n, k in enumerate(steps):
            for i in both:
                sums[k, i] = result[2 * n + i]
        return [result]

    def tie(k, *others):
        got[k] = lax.optimization_barrier((*got[k], *others))[:2]

    later(1)
    begun = jnp.pad(unpack(start)[:pair], ((size, 8), (0, 0)))
    sent[1] = [pack(sums[1, 0] + begun, jnp.maximum(top, tag_of(start))), pack(sums[1, 1], top)]
    got[1] = send(sent[1])
    tie(2, *later(3, 4))
    kept = {}
    for k in (4, 3, 6, 5, 7):
        before = [unpack(got[k - 2][i]) for i in both]
        value = [sums[k, i] + before[i] for i in both]
        level = [jnp.maximum(top, tag_of(got[k - 2][i])) for i in both]
        if k == 5:
            kept[2] = [v[size : size + pair] for v in value]
        if k == 7:
            even = [unpack(got[6][i]) for i in both]
            kept[1] = [(sums[8, i] + even[i])[size : size + pair] for i in both]
            own = [sums[8, i][:size] + even[1 - i][:size] for i in both]
            level = [jnp.maximum(level[i], tag_of(got[6][i])) for i in both]
            room = jnp.zeros((16, LANES), jnp.float32)
            value = [jnp.concatenate([value[i][:-8], kept[1][i], room], 0) for i in both]
        sent[k] = [pack(value[i], level[i]) for i in both]
        got[k] = send(sent[k])
        if k == 4:
            tie(1, *later(5, 6))
        elif k == 3:
            tie(4, *later(7, 8))
        elif k < 7:
            tie(9 - k if k == 6 else k + 1, *sent[k])

    factor = 1.0 / (tokens * DP)
    end = [unpack(got[7][i]) for i in both]
    return finish(me.reshape(1), own, kept[1], kept[2], end, rows, factor)[None]


def solution(mesh):
    return jax.shard_map(
        on_device,
        mesh=mesh,
        in_specs=(
            P("section", "dp", "tensor"),
            P("section", "tensor"),
            P("section", "dp", "tensor"),
        ),
        out_specs=P("section", ("tensor", "dp"), None),
        check_vma=False,
    )
```

profile of v0, /device:TPU:8, one launch (start us, length us, event | category | flops | bytes accessed | tf_op | source)
XLA Modules:
  0.0 111.2 jit_solution(6242058698923175827)
XLA Ops:
  0.0 1.2 %copy-done = bf16[1,1024,512]{2,1,0:T(8,128)(2,1)S(1)} copy-done((bf16[1,1024,512]{2,1,0:T(8,128)(2,1)S(1)}, bf16[1,1024,512]{2,1,0:T(8,128)(2,1)}, u32[]{:S(2)}) %copy-start) | copy-done | bytes 1048600
  1.9 1.0 shard_map.82
  3.0 4.2 %collective-permute-start.1 = (bf16[464,512]{1,0:T(8,128)(2,1)}, bf16[464,512]{1,0:T(8,128)(2,1)}, u32[]{:S(2)}, u32[]{:S(2)}) collective-permute-start(bf16[464,512]{1,0:T(8,128)(2,1)} %get-tuple-element.30), channel_id=1, source_target_pairs={{0,128},{1,129},{2,130},{3,131},{4,132},{5,133},{6,134},{7,135},{8... | collective-permute-start | bytes 1425416 | tf_op jit(solution)/shard_map/ppermute | solution.py:79
  7.1 1.3 %collective-permute-start = (bf16[576,512]{1,0:T(8,128)(2,1)}, bf16[576,512]{1,0:T(8,128)(2,1)S(1)}, u32[]{:S(2)}, u32[]{:S(2)}) collective-permute-start(bf16[576,512]{1,0:T(8,128)(2,1)} %get-tuple-element.29), channel_id=1, source_target_pairs={{128,0},{129,1},{130,2},{131,3},{132,4},{133,5},{134,6},{135,7},{1... | collective-permute-start | bytes 1769480 | tf_op jit(solution)/shard_map/ppermute | solution.py:80
  8.9 2.9 %copy.11 = bf16[1,1024,896]{1,2,0:T(8,128)(2,1)S(1)} copy(bf16[1,1024,896]{2,1,0:T(8,128)(2,1)} %param.10) | data formatting | bytes 3670016 | tf_op args[2]
  13.1 3.0 %fusion.turned_ref = bf16[896,1024]{1,0:T(8,128)(2,1)S(1)} fusion(s32[]{:T(128)S(6)} %select_n.60, bf16[896,1024]{1,0:T(8,128)(2,1)} %bitcast.205), kind=kLoop, calls=%fused_computation.2 | loop fusion | flops 3670016 | bytes 3670020 | tf_op jit(solution)/shard_map/concatenate | solution.py:255
  16.8 1.6 %shard_map.85 = f32[4,448]{1,0:T(4,128)S(1)} custom-call(s32[1,512]{1,0:T(1,128)S(1)} %copy-done.3, bf16[1024,512]{1,0:T(8,128)(2,1)S(1)} %bitcast.202, bf16[464,512]{1,0:T(8,128)(2,1)} %collective-permute-done.1.refs_0_), custom_call_target="tpu_custom_call" | custom-call | tf_op jit(solution)/shard_map/pallas_call | solution.py:69
  18.4 1.4 %collective-permute-start.2 = (f32[4,448]{1,0:T(4,128)S(1)}, f32[4,448]{1,0:T(4,128)S(1)}, u32[]{:S(2)}, u32[]{:S(2)}) collective-permute-start(f32[4,448]{1,0:T(4,128)S(1)} %shard_map.85), channel_id=1, source_target_pairs={{128,0},{129,1},{130,2},{131,3},{132,4},{133,5},{134,6},{135,7},{1... | collective-permute-start | bytes 21512 | tf_op jit(solution)/shard_map/ppermute | solution.py:84
  19.8 4.4 %collective-permute-done.2 = f32[4,448]{1,0:T(4,128)S(1)} collective-permute-done((f32[4,448]{1,0:T(4,128)S(1)}, f32[4,448]{1,0:T(4,128)S(1)}, u32[]{:S(2)}, u32[]{:S(2)}) %collective-permute-start.2) | collective-permute-done | bytes 7200 | tf_op jit(solution)/shard_map/ppermute | solution.py:84
  25.0 1.2 %collective-permute-done.3 = f32[4,1024]{1,0:T(4,128)S(1)} collective-permute-done((f32[4,1024]{1,0:T(4,128)S(1)}, f32[4,1024]{1,0:T(4,128)S(1)}, u32[]{:S(2)}, u32[]{:S(2)}) %collective-permute-start.3) | collective-permute-done | bytes 16416 | tf_op jit(solution)/shard_map/ppermute | solution.py:88
  26.9 7.1 %all-to-all-start = ((f32[8,4,1024]{2,1,0:T(4,128)}), f32[8,4,1024]{2,1,0:T(4,128)S(1)}, u32[]{:S(2)}, u32[]{:S(2)}) async-start(f32[8,4,1024]{2,1,0:T(4,128)} %broadcast_in_dim.117), calls=%async_computation | async-start | bytes 262144 | tf_op jit(solution)/shard_map/all_to_all | solution.py:91
  34.1 6.5 %all-to-all-done = f32[8,4,1024]{2,1,0:T(4,128)S(1)} async-done(((f32[8,4,1024]{2,1,0:T(4,128)}), f32[8,4,1024]{2,1,0:T(4,128)S(1)}, u32[]{:S(2)}, u32[]{:S(2)}) %all-to-all-start) | async-done | bytes 131104 | tf_op jit(solution)/shard_map/all_to_all | solution.py:91
  41.6 2.0 %collective-permute-start.4 = (f16[400,128]{1,0:T(8,128)(2,1)S(1)}, f16[400,128]{1,0:T(8,128)(2,1)S(1)}, u32[]{:S(2)}, u32[]{:S(2)}) collective-permute-start(f16[400,128]{1,0:T(8,128)(2,1)S(1)} %select_convert_fusion.2), channel_id=1, source_target_pairs={{0,16},{16,32},{32,48},{48,64},{64,80},{80,96},{96,112},{112,0},{1... | collective-permute-start | bytes 307208 | tf_op jit(solution)/shard_map/ppermute | solution.py:23
  43.6 3.8 %shard_map.86 = (bf16[4,896,1024]{2,1,0:T(8,128)(2,1)S(1)}, f32[2,1184,128]{2,1,0:T(8,128)S(1)}) custom-call(s32[2,4]{1,0:T(2,128)S(1)} %copy-done.7, f32[4,1024]{1,0:T(4,128)S(1)} %broadcast_multiply_fusion.factors_ref.weight_ref, bf16[896,1024]{1,0:T(8,128)(2,1)S(1)} %fusion.turned_ref), custom_call_target="tpu_custom_call" | custom-call | flops 1 | bytes 1 | tf_op jit(solution)/shard_map/pallas_call | solution.py:188
  47.6 2.0 %collective-permute-start.5 = (f16[1184,128]{1,0:T(8,128)(2,1)S(1)}, f16[1184,128]{1,0:T(8,128)(2,1)S(1)}, u32[]{:S(2)}, u32[]{:S(2)}) collective-permute-start(f16[1184,128]{1,0:T(8,128)(2,1)S(1)} %get-tuple-element.76), channel_id=1, source_target_pairs={{0,16},{16,32},{32,48},{48,64},{64,80},{80,96},{96,112},{112,0},{1... | collective-permute-start | bytes 909320 | tf_op jit(solution)/shard_map/ppermute | solution.py:23
  49.6 2.3 %collective-permute-start.6 = (f16[1184,128]{1,0:T(8,128)(2,1)S(1)}, f16[1184,128]{1,0:T(8,128)(2,1)S(1)}, u32[]{:S(2)}, u32[]{:S(2)}) collective-permute-start(f16[1184,128]{1,0:T(8,128)(2,1)S(1)} %get-tuple-element.75), channel_id=1, source_target_pairs={{0,112},{16,0},{32,16},{48,32},{64,48},{80,64},{96,80},{112,96},{1... | collective-permute-start | bytes 909320 | tf_op jit(solution)/shard_map/ppermute | solution.py:23
  51.9 2.8 %shard_map.88 = f32[2,1184,128]{2,1,0:T(8,128)S(1)} custom-call(s32[2,4]{1,0:T(2,128)S(1)} %copy-done.8, bf16[4,896,1024]{2,1,0:T(8,128)(2,1)S(1)} %get-tuple-element.46.factors_ref, bf16[896,1024]{1,0:T(8,128)(2,1)S(1)} %fusion.turned_ref), custom_call_target="tpu_custom_call" | custom-call | flops 1 | bytes 1 | tf_op jit(solution)/shard_map/pallas_call | solution.py:188
  55.2 3.2 %collective-permute-start.8 = (f16[1184,128]{1,0:T(8,128)(2,1)S(1)}, f16[1184,128]{1,0:T(8,128)(2,1)S(1)}, u32[]{:S(2)}, u32[]{:S(2)}) collective-permute-start(f16[1184,128]{1,0:T(8,128)(2,1)S(1)} %get-tuple-element.77), channel_id=1, source_target_pairs={{0,112},{16,0},{32,16},{48,32},{64,48},{80,64},{96,80},{112,96},{1... | collective-permute-start | bytes 909320 | tf_op jit(solution)/shard_map/ppermute | solution.py:23
  58.4 5.1 %shard_map.89 = f32[4,1184,128]{2,1,0:T(8,128)S(1)} custom-call(s32[4,4]{1,0:T(4,128)S(1)} %copy-done.6, bf16[4,896,1024]{2,1,0:T(8,128)(2,1)S(1)} %get-tuple-element.46.factors_ref, bf16[896,1024]{1,0:T(8,128)(2,1)S(1)} %fusion.turned_ref), custom_call_target="tpu_custom_call" | custom-call | flops 1 | bytes 1 | tf_op jit(solution)/shard_map/pallas_call | solution.py:188
  64.8 1.2 %collective-permute-start.9 = (f16[1184,128]{1,0:T(8,128)(2,1)S(1)}, f16[1184,128]{1,0:T(8,128)(2,1)S(1)}, u32[]{:S(2)}, u32[]{:S(2)}) collective-permute-start(f16[1184,128]{1,0:T(8,128)(2,1)S(1)} %get-tuple-element.68), channel_id=1, source_target_pairs={{0,16},{16,32},{32,48},{48,64},{64,80},{80,96},{96,112},{112,0},{1... | collective-permute-start | bytes 909320 | tf_op jit(solution)/shard_map/ppermute | solution.py:23
  66.1 5.1 %shard_map.90 = f32[4,1184,128]{2,1,0:T(8,128)S(1)} custom-call(s32[4,4]{1,0:T(4,128)S(1)} %copy-done.5, bf16[4,896,1024]{2,1,0:T(8,128)(2,1)S(1)} %get-tuple-element.46.factors_ref, bf16[896,1024]{1,0:T(8,128)(2,1)S(1)} %fusion.turned_ref), custom_call_target="tpu_custom_call" | custom-call | flops 1 | bytes 1 | tf_op jit(solution)/shard_map/pallas_call | solution.py:188
  71.7 3.2 %collective-permute-start.14 = (f16[1184,128]{1,0:T(8,128)(2,1)S(1)}, f16[1184,128]{1,0:T(8,128)(2,1)S(1)}, u32[]{:S(2)}, u32[]{:S(2)}) collective-permute-start(f16[1184,128]{1,0:T(8,128)(2,1)S(1)} %get-tuple-element.65), channel_id=1, source_target_pairs={{0,112},{16,0},{32,16},{48,32},{64,48},{80,64},{96,80},{112,96},{1... | collective-permute-start | bytes 909320 | tf_op jit(solution)/shard_map/ppermute | solution.py:23
  74.9 5.1 %shard_map.91 = f32[4,1184,128]{2,1,0:T(8,128)S(1)} custom-call(s32[4,4]{1,0:T(4,128)S(1)} %copy-done.4, bf16[4,896,1024]{2,1,0:T(8,128)(2,1)S(1)} %get-tuple-element.46.factors_ref, bf16[896,1024]{1,0:T(8,128)(2,1)S(1)} %fusion.turned_ref), custom_call_target="tpu_custom_call" | custom-call | flops 1 | bytes 1 | tf_op jit(solution)/shard_map/pallas_call | solution.py:188
  80.5 3.2 %collective-permute-start.12 = (f16[1184,128]{1,0:T(8,128)(2,1)S(1)}, f16[1184,128]{1,0:T(8,128)(2,1)S(1)}, u32[]{:S(2)}, u32[]{:S(2)}) collective-permute-start(f16[1184,128]{1,0:T(8,128)(2,1)S(1)} %get-tuple-element.63), channel_id=1, source_target_pairs={{0,112},{16,0},{32,16},{48,32},{64,48},{80,64},{96,80},{112,96},{1... | collective-permute-start | bytes 909320 | tf_op jit(solution)/shard_map/ppermute | solution.py:23
  84.2 3.2 %collective-permute-start.17 = (f16[1184,128]{1,0:T(8,128)(2,1)S(1)}, f16[1184,128]{1,0:T(8,128)(2,1)S(1)}, u32[]{:S(2)}, u32[]{:S(2)}) collective-permute-start(f16[1184,128]{1,0:T(8,128)(2,1)S(1)} %get-tuple-element.57), channel_id=1, source_target_pairs={{0,112},{16,0},{32,16},{48,32},{64,48},{80,64},{96,80},{112,96},{1... | collective-permute-start | bytes 909320 | tf_op jit(solution)/shard_map/ppermute | solution.py:23
  87.6 3.3 %collective-permute-done.11 = f16[1184,128]{1,0:T(8,128)(2,1)S(1)} collective-permute-done((f16[1184,128]{1,0:T(8,128)(2,1)S(1)}, f16[1184,128]{1,0:T(8,128)(2,1)S(1)}, u32[]{:S(2)}, u32[]{:S(2)}) %collective-permute-start.11) | collective-permute-done | bytes 303136 | tf_op jit(solution)/shard_map/ppermute | solution.py:23
  90.8 3.2 %collective-permute-done.15 = f16[1184,128]{1,0:T(8,128)(2,1)S(1)} collective-permute-done((f16[1184,128]{1,0:T(8,128)(2,1)S(1)}, f16[1184,128]{1,0:T(8,128)(2,1)S(1)}, u32[]{:S(2)}, u32[]{:S(2)}) %collective-permute-start.15) | collective-permute-done | bytes 303136 | tf_op jit(solution)/shard_map/ppermute | solution.py:23
  94.4 1.5 %fusion.4 = (f16[1584,128]{1,0:T(8,128)(2,1)S(1)}, f16[1584,128]{1,0:T(8,128)(2,1)S(1)}) fusion(f32[392,128]{1,0:T(8,128)S(1)} %slice_add_fusion.4.refs_3_, f32[1176,128]{1,0:T(8,128)S(1)} %get-tuple-element.132, f32[1584]{0:T(1024)S(1)} %pad.10.clone, f32[128]{0:T(128)S(1)} %get-tuple-element.53, f32[128]{0:T(128)S(1)} %bitcast.206, ...), kind=kLoop, calls=%fused_computation.9 | loop fusion | flops 2027520 | bytes 2426608 | tf_op jit(solution)/shard_map/convert_element_type | solution.py:271
  96.0 3.0 %collective-permute-start.18 = (f16[1584,128]{1,0:T(8,128)(2,1)S(1)}, f16[1584,128]{1,0:T(8,128)(2,1)S(1)}, u32[]{:S(2)}, u32[]{:S(2)}) collective-permute-start(f16[1584,128]{1,0:T(8,128)(2,1)S(1)} %get-tuple-element.110), channel_id=1, source_target_pairs={{0,112},{16,0},{32,16},{48,32},{64,48},{80,64},{96,80},{112,96},{1... | collective-permute-start | bytes 1216520 | tf_op jit(solution)/shard_map/ppermute | solution.py:23
  99.2 5.2 %collective-permute-done.18 = f16[1584,128]{1,0:T(8,128)(2,1)S(1)} collective-permute-done((f16[1584,128]{1,0:T(8,128)(2,1)S(1)}, f16[1584,128]{1,0:T(8,128)(2,1)S(1)}, u32[]{:S(2)}, u32[]{:S(2)}) %collective-permute-start.18) | collective-permute-done | bytes 405536 | tf_op jit(solution)/shard_map/ppermute | solution.py:23
  104.5 3.7 %collective-permute-done.16 = f16[1584,128]{1,0:T(8,128)(2,1)S(1)} collective-permute-done((f16[1584,128]{1,0:T(8,128)(2,1)S(1)}, f16[1584,128]{1,0:T(8,128)(2,1)S(1)}, u32[]{:S(2)}, u32[]{:S(2)}) %collective-permute-start.16) | collective-permute-done | bytes 405536 | tf_op jit(solution)/shard_map/ppermute | solution.py:23
  108.3 2.9 %shard_map.92 = f32[112,3584]{1,0:T(8,128)} custom-call(s32[1]{0:T(128)} %bitcast.me_ref, f32[784,128]{1,0:T(8,128)S(1)} %get-tuple-element.74.refs_0_, f32[784,128]{1,0:T(8,128)S(1)} %get-tuple-element.73.refs_1_, f32[392,128]{1,0:T(8,128)S(1)} %slice_add_fusion.5.refs_2_, f32[392,128]{1,0:T(8,128)S(1)} %slice_add_fusion.4.refs_3_, ...), custom_call_target="tpu_custom_call" | custom-call | tf_op jit(solution)/shard_map/pallas_call | solution.py:239
  (82 shorter events, 9.7 us)
Async XLA Ops:
  0.0 1.2 %copy-start = (bf16[1,1024,512]{2,1,0:T(8,128)(2,1)S(1)}, bf16[1,1024,512]{2,1,0:T(8,128)(2,1)}, u32[]{:S(2)}) copy-start(bf16[1,1024,512]{2,1,0:T(8,128)(2,1)} %param.8) | copy-start | bytes 3145732
  1.2 0.7 copy-start.2
  3.0 13.8 %collective-permute-start.1 = (bf16[464,512]{1,0:T(8,128)(2,1)}, bf16[464,512]{1,0:T(8,128)(2,1)}, u32[]{:S(2)}, u32[]{:S(2)}) collective-permute-start(bf16[464,512]{1,0:T(8,128)(2,1)} %get-tuple-element.30), channel_id=1, source_target_pairs={{0,128},{1,129},{2,130},{3,131},{4,132},{5,133},{6,134},{7,135},{8... | collective-permute-start | bytes 1425416 | tf_op jit(solution)/shard_map/ppermute | solution.py:79
  7.1 17.1 %collective-permute-start = (bf16[576,512]{1,0:T(8,128)(2,1)}, bf16[576,512]{1,0:T(8,128)(2,1)S(1)}, u32[]{:S(2)}, u32[]{:S(2)}) collective-permute-start(bf16[576,512]{1,0:T(8,128)(2,1)} %get-tuple-element.29), channel_id=1, source_target_pairs={{128,0},{129,1},{130,2},{131,3},{132,4},{133,5},{134,6},{135,7},{1... | collective-permute-start | bytes 1769480 | tf_op jit(solution)/shard_map/ppermute | solution.py:80
  11.9 1.3 %copy-start.9 = (bf16[1,1024,896]{1,2,0:T(8,128)(2,1)}, bf16[1,1024,896]{1,2,0:T(8,128)(2,1)S(1)}, u32[]{:S(2)}) copy-start(bf16[1,1024,896]{1,2,0:T(8,128)(2,1)S(1)} %copy.11) | copy-start | bytes 5505028
  11.9 4.9 %copy-start.1 = (bf16[1,1024,512]{2,1,0:T(8,128)(2,1)S(1)}, bf16[1,1024,512]{2,1,0:T(8,128)(2,1)}, u32[]{:S(2)}) copy-start(bf16[1,1024,512]{2,1,0:T(8,128)(2,1)} %param.8) | copy-start | bytes 3145732
  11.9 4.9 %copy-start.3 = (s32[1,512]{1,0:T(1,128)S(1)}, s32[1,512]{1,0:T(1,128)}, u32[]{:S(2)}) copy-start(s32[1,512]{1,0:T(1,128)} %groups_ref.7) | copy-start | bytes 6148
  18.3 25.2 %copy-start.7 = (s32[2,4]{1,0:T(2,128)S(1)}, s32[2,4]{1,0:T(2,128)}, u32[]{:S(2)}) copy-start(s32[2,4]{1,0:T(2,128)} %constant.62.clone.table_ref) | copy-start | bytes 100
  18.4 5.8 %collective-permute-start.2 = (f32[4,448]{1,0:T(4,128)S(1)}, f32[4,448]{1,0:T(4,128)S(1)}, u32[]{:S(2)}, u32[]{:S(2)}) collective-permute-start(f32[4,448]{1,0:T(4,128)S(1)} %shard_map.85), channel_id=1, source_target_pairs={{128,0},{129,1},{130,2},{131,3},{132,4},{133,5},{134,6},{135,7},{1... | collective-permute-start | bytes 21512 | tf_op jit(solution)/shard_map/ppermute | solution.py:84
  25.0 1.2 %collective-permute-start.3 = (f32[4,1024]{1,0:T(4,128)S(1)}, f32[4,1024]{1,0:T(4,128)S(1)}, u32[]{:S(2)}, u32[]{:S(2)}) collective-permute-start(f32[4,1024]{1,0:T(4,128)S(1)} %pad_maximum_fusion), channel_id=1, source_target_pairs={{0,1},{1,0},{2,3},{3,2},{4,5},{5,4},{6,7},{7,6},{8,9},{9,8},{10,11... | collective-permute-start | bytes 49160 | tf_op jit(solution)/shard_map/ppermute | solution.py:88
  26.9 13.7 %all-to-all-start = ((f32[8,4,1024]{2,1,0:T(4,128)}), f32[8,4,1024]{2,1,0:T(4,128)S(1)}, u32[]{:S(2)}, u32[]{:S(2)}) async-start(f32[8,4,1024]{2,1,0:T(4,128)} %broadcast_in_dim.117), calls=%async_computation | async-start | bytes 262144 | tf_op jit(solution)/shard_map/all_to_all | solution.py:91
  41.4 10.5 %copy-start.8 = (s32[2,4]{1,0:T(2,128)S(1)}, s32[2,4]{1,0:T(2,128)}, u32[]{:S(2)}) copy-start(s32[2,4]{1,0:T(2,128)} %constant.63.clone.table_ref) | copy-start | bytes 100
  41.6 13.2 %collective-permute-start.4 = (f16[400,128]{1,0:T(8,128)(2,1)S(1)}, f16[400,128]{1,0:T(8,128)(2,1)S(1)}, u32[]{:S(2)}, u32[]{:S(2)}) collective-permute-start(f16[400,128]{1,0:T(8,128)(2,1)S(1)} %select_convert_fusion.2), channel_id=1, source_target_pairs={{0,16},{16,32},{32,48},{48,64},{64,80},{80,96},{96,112},{112,0},{1... | collective-permute-start | bytes 307208 | tf_op jit(solution)/shard_map/ppermute | solution.py:23
  47.6 15.9 %collective-permute-start.5 = (f16[1184,128]{1,0:T(8,128)(2,1)S(1)}, f16[1184,128]{1,0:T(8,128)(2,1)S(1)}, u32[]{:S(2)}, u32[]{:S(2)}) collective-permute-start(f16[1184,128]{1,0:T(8,128)(2,1)S(1)} %get-tuple-element.76), channel_id=1, source_target_pairs={{0,16},{16,32},{32,48},{48,64},{64,80},{80,96},{96,112},{112,0},{1... | collective-permute-start | bytes 909320 | tf_op jit(solution)/shard_map/ppermute | solution.py:23
  49.6 14.0 %collective-permute-start.6 = (f16[1184,128]{1,0:T(8,128)(2,1)S(1)}, f16[1184,128]{1,0:T(8,128)(2,1)S(1)}, u32[]{:S(2)}, u32[]{:S(2)}) collective-permute-start(f16[1184,128]{1,0:T(8,128)(2,1)S(1)} %get-tuple-element.75), channel_id=1, source_target_pairs={{0,112},{16,0},{32,16},{48,32},{64,48},{80,64},{96,80},{112,96},{1... | collective-permute-start | bytes 909320 | tf_op jit(solution)/shard_map/ppermute | solution.py:23
  51.9 6.5 %copy-start.6 = (s32[4,4]{1,0:T(4,128)S(1)}, s32[4,4]{1,0:T(4,128)}, u32[]{:S(2)}) copy-start(s32[4,4]{1,0:T(4,128)} %constant.64.clone.table_ref) | copy-start | bytes 196
  55.1 16.1 %collective-permute-start.7 = (f16[1184,128]{1,0:T(8,128)(2,1)S(1)}, f16[1184,128]{1,0:T(8,128)(2,1)S(1)}, u32[]{:S(2)}, u32[]{:S(2)}) collective-permute-start(f16[1184,128]{1,0:T(8,128)(2,1)S(1)} %get-tuple-element.78), channel_id=1, source_target_pairs={{0,16},{16,32},{32,48},{48,64},{64,80},{80,96},{96,112},{112,0},{1... | collective-permute-start | bytes 909320 | tf_op jit(solution)/shard_map/ppermute | solution.py:23
  55.2 16.0 %collective-permute-start.8 = (f16[1184,128]{1,0:T(8,128)(2,1)S(1)}, f16[1184,128]{1,0:T(8,128)(2,1)S(1)}, u32[]{:S(2)}, u32[]{:S(2)}) collective-permute-start(f16[1184,128]{1,0:T(8,128)(2,1)S(1)} %get-tuple-element.77), channel_id=1, source_target_pairs={{0,112},{16,0},{32,16},{48,32},{64,48},{80,64},{96,80},{112,96},{1... | collective-permute-start | bytes 909320 | tf_op jit(solution)/shard_map/ppermute | solution.py:23
  63.5 2.5 %copy-start.5 = (s32[4,4]{1,0:T(4,128)S(1)}, s32[4,4]{1,0:T(4,128)}, u32[]{:S(2)}) copy-start(s32[4,4]{1,0:T(4,128)} %constant.65.clone.table_ref) | copy-start | bytes 196
  64.0 16.1 %collective-permute-start.10 = (f16[1184,128]{1,0:T(8,128)(2,1)S(1)}, f16[1184,128]{1,0:T(8,128)(2,1)S(1)}, u32[]{:S(2)}, u32[]{:S(2)}) collective-permute-start(f16[1184,128]{1,0:T(8,128)(2,1)S(1)} %get-tuple-element.67), channel_id=1, source_target_pairs={{0,112},{16,0},{32,16},{48,32},{64,48},{80,64},{96,80},{112,96},{1... | collective-permute-start | bytes 909320 | tf_op jit(solution)/shard_map/ppermute | solution.py:23
  64.8 15.3 %collective-permute-start.9 = (f16[1184,128]{1,0:T(8,128)(2,1)S(1)}, f16[1184,128]{1,0:T(8,128)(2,1)S(1)}, u32[]{:S(2)}, u32[]{:S(2)}) collective-permute-start(f16[1184,128]{1,0:T(8,128)(2,1)S(1)} %get-tuple-element.68), channel_id=1, source_target_pairs={{0,16},{16,32},{32,48},{48,64},{64,80},{80,96},{96,112},{112,0},{1... | collective-permute-start | bytes 909320 | tf_op jit(solution)/shard_map/ppermute | solution.py:23
  71.2 3.7 %copy-start.4 = (s32[4,4]{1,0:T(4,128)S(1)}, s32[4,4]{1,0:T(4,128)}, u32[]{:S(2)}) copy-start(s32[4,4]{1,0:T(4,128)} %constant.66.clone.table_ref) | copy-start | bytes 196
  71.6 12.2 %collective-permute-start.13 = (f16[1184,128]{1,0:T(8,128)(2,1)S(1)}, f16[1184,128]{1,0:T(8,128)(2,1)S(1)}, u32[]{:S(2)}, u32[]{:S(2)}) collective-permute-start(f16[1184,128]{1,0:T(8,128)(2,1)S(1)} %get-tuple-element.66), channel_id=1, source_target_pairs={{0,16},{16,32},{32,48},{48,64},{64,80},{80,96},{96,112},{112,0},{1... | collective-permute-start | bytes 909320 | tf_op jit(solution)/shard_map/ppermute | solution.py:23
  71.7 12.1 %collective-permute-start.14 = (f16[1184,128]{1,0:T(8,128)(2,1)S(1)}, f16[1184,128]{1,0:T(8,128)(2,1)S(1)}, u32[]{:S(2)}, u32[]{:S(2)}) collective-permute-start(f16[1184,128]{1,0:T(8,128)(2,1)S(1)} %get-tuple-element.65), channel_id=1, source_target_pairs={{0,112},{16,0},{32,16},{48,32},{64,48},{80,64},{96,80},{112,96},{1... | collective-permute-start | bytes 909320 | tf_op jit(solution)/shard_map/ppermute | solution.py:23
  80.4 10.4 %collective-permute-start.11 = (f16[1184,128]{1,0:T(8,128)(2,1)S(1)}, f16[1184,128]{1,0:T(8,128)(2,1)S(1)}, u32[]{:S(2)}, u32[]{:S(2)}) collective-permute-start(f16[1184,128]{1,0:T(8,128)(2,1)S(1)} %get-tuple-element.64), channel_id=1, source_target_pairs={{0,16},{16,32},{32,48},{48,64},{64,80},{80,96},{96,112},{112,0},{1... | collective-permute-start | bytes 909320 | tf_op jit(solution)/shard_map/ppermute | solution.py:23
  80.5 10.3 %collective-permute-start.12 = (f16[1184,128]{1,0:T(8,128)(2,1)S(1)}, f16[1184,128]{1,0:T(8,128)(2,1)S(1)}, u32[]{:S(2)}, u32[]{:S(2)}) collective-permute-start(f16[1184,128]{1,0:T(8,128)(2,1)S(1)} %get-tuple-element.63), channel_id=1, source_target_pairs={{0,112},{16,0},{32,16},{48,32},{64,48},{80,64},{96,80},{112,96},{1... | collective-permute-start | bytes 909320 | tf_op jit(solution)/shard_map/ppermute | solution.py:23
  84.1 10.0 %collective-permute-start.15 = (f16[1184,128]{1,0:T(8,128)(2,1)S(1)}, f16[1184,128]{1,0:T(8,128)(2,1)S(1)}, u32[]{:S(2)}, u32[]{:S(2)}) collective-permute-start(f16[1184,128]{1,0:T(8,128)(2,1)S(1)} %get-tuple-element.61), channel_id=1, source_target_pairs={{0,16},{16,32},{32,48},{48,64},{64,80},{80,96},{96,112},{112,0},{1... | collective-permute-start | bytes 909320 | tf_op jit(solution)/shard_map/ppermute | solution.py:23
  84.2 9.9 %collective-permute-start.17 = (f16[1184,128]{1,0:T(8,128)(2,1)S(1)}, f16[1184,128]{1,0:T(8,128)(2,1)S(1)}, u32[]{:S(2)}, u32[]{:S(2)}) collective-permute-start(f16[1184,128]{1,0:T(8,128)(2,1)S(1)} %get-tuple-element.57), channel_id=1, source_target_pairs={{0,112},{16,0},{32,16},{48,32},{64,48},{80,64},{96,80},{112,96},{1... | collective-permute-start | bytes 909320 | tf_op jit(solution)/shard_map/ppermute | solution.py:23
  96.0 8.5 %collective-permute-start.18 = (f16[1584,128]{1,0:T(8,128)(2,1)S(1)}, f16[1584,128]{1,0:T(8,128)(2,1)S(1)}, u32[]{:S(2)}, u32[]{:S(2)}) collective-permute-start(f16[1584,128]{1,0:T(8,128)(2,1)S(1)} %get-tuple-element.110), channel_id=1, source_target_pairs={{0,112},{16,0},{32,16},{48,32},{64,48},{80,64},{96,80},{112,96},{1... | collective-permute-start | bytes 1216520 | tf_op jit(solution)/shard_map/ppermute | solution.py:23
  99.0 9.2 %collective-permute-start.16 = (f16[1584,128]{1,0:T(8,128)(2,1)S(1)}, f16[1584,128]{1,0:T(8,128)(2,1)S(1)}, u32[]{:S(2)}, u32[]{:S(2)}) collective-permute-start(f16[1584,128]{1,0:T(8,128)(2,1)S(1)} %get-tuple-element.111), channel_id=1, source_target_pairs={{0,16},{16,32},{32,48},{48,64},{64,80},{80,96},{96,112},{112,0},{1... | collective-permute-start | bytes 1216520 | tf_op jit(solution)/shard_map/ppermute | solution.py:23
where the time goes:
time: 112 us; the launch traced here: 111 us
  starting transfers between devices  38.8 us (35%)
  Pallas kernels  29.5 us (26%)
  waiting for transfers between devices  28.1 us (25%)
  other arithmetic  7.6 us (7%)
  local copies, waits for them, and re-layouts  6.82 us (6%)
    ppermute x15, starting transfers between devices, shift(): lax.ppermute(value, axis, [(i, (i + steps) % count) for i in range(count)])  24.7 us
    pallas_call x5, Pallas kernels, products(): pl.pallas_call(functools.partial(product_kernel, make), in_specs=[pl.Bloc...  22 us
    ppermute x15, waiting for transfers between devices, shift(): lax.ppermute(value, axis, [(i, (i + steps) % count) for i in range(count)])  15.5 us
    all_to_all x1, starting transfers between devices, section_weights(): lax.all_to_all(spread, 'tensor', 0, 0, axis_index_groups=chips, tiled=True)  7.08 us
    all_to_all x1, waiting for transfers between devices, section_weights(): lax.all_to_all(spread, 'tensor', 0, 0, axis_index_groups=chips, tiled=True)  6.48 us
    unnamed x21, local copies, waits for them, and re-layouts  5.88 us
    ppermute x1, waiting for transfers between devices, section_weights(): back = lax.ppermute(back, 'section', [(1, 0)])  4.39 us
    ppermute x1, starting transfers between devices, section_weights(): first = lax.ppermute(moved, 'section', [(0, 1)])  4.17 us
  transfers between devices with their start and end apart: 20, of which 8 were waited for; matrix products, arithmetic and copies ran while one was open for 8% of the time, Pallas kernels for 22%

commit v1 on v0

--- a/solution.py
+++ b/solution.py
@@ -325,9 +325,11 @@
         sent[k] = [pack(value[i], level[i]) for i in both]
         got[k] = send(sent[k])
         if k == 4:
-            tie(1, *later(5, 6))
+            tie(1, *sent[k])
         elif k == 3:
-            tie(4, *later(7, 8))
+            tie(4, *later(5, 6))
+        elif k == 6:
+            tie(3, *later(7, 8))
         elif k < 7:
             tie(9 - k if k == 6 else k + 1, *sent[k])
 

time: 112 us -> 111 us (level)
    ppermute x15, waiting for transfers between devices: 15.5 us -> 14.3 us  [shift(): lax.ppermute(value, axis, [(i, (i + steps) % count) for i in range(count)])]
where the time goes in v1:
time: 111 us; the launch traced here: 110 us
  starting transfers between devices  39.1 us (35%)
  Pallas kernels  29.5 us (27%)
  waiting for transfers between devices  27 us (24%)
  other arithmetic  7.62 us (7%)
  local copies, waits for them, and re-layouts  6.82 us (6%)
    ppermute x15, starting transfers between devices, shift(): lax.ppermute(value, axis, [(i, (i + steps) % count) for i in range(count)])  25 us
    pallas_call x5, Pallas kernels, products(): pl.pallas_call(functools.partial(product_kernel, make), in_specs=[pl.Bloc...  22 us
    ppermute x15, waiting for transfers between devices, shift(): lax.ppermute(value, axis, [(i, (i + steps) % count) for i in range(count)])  14.3 us
    all_to_all x1, starting transfers between devices, section_weights(): lax.all_to_all(spread, 'tensor', 0, 0, axis_index_groups=chips, tiled=True)  7.08 us
    all_to_all x1, waiting for transfers between devices, section_weights(): lax.all_to_all(spread, 'tensor', 0, 0, axis_index_groups=chips, tiled=True)  6.48 us
    unnamed x21, local copies, waits for them, and re-layouts  5.88 us
    ppermute x1, waiting for transfers between devices, section_weights(): back = lax.ppermute(back, 'section', [(1, 0)])  4.39 us
    ppermute x1, starting transfers between devices, section_weights(): first = lax.ppermute(moved, 'section', [(0, 1)])  4.17 us
  transfers between devices with their start and end apart: 20, of which 8 were waited for; matrix products, arithmetic and copies ran while one was open for 8% of the time, Pallas kernels for 22%

profile of v1, /device:TPU:8, one launch (start us, length us, event | category | flops | bytes accessed | tf_op | source)
XLA Modules:
  0.0 110.4 jit_solution(8412413366835616007)
XLA Ops:
  0.0 1.2 %copy-done = bf16[1,1024,512]{2,1,0:T(8,128)(2,1)S(1)} copy-done((bf16[1,1024,512]{2,1,0:T(8,128)(2,1)S(1)}, bf16[1,1024,512]{2,1,0:T(8,128)(2,1)}, u32[]{:S(2)}) %copy-start) | copy-done | bytes 1048600
  1.9 1.0 shard_map.82
  3.0 4.2 %collective-permute-start.1 = (bf16[464,512]{1,0:T(8,128)(2,1)}, bf16[464,512]{1,0:T(8,128)(2,1)}, u32[]{:S(2)}, u32[]{:S(2)}) collective-permute-start(bf16[464,512]{1,0:T(8,128)(2,1)} %get-tuple-element.30), channel_id=1, source_target_pairs={{0,128},{1,129},{2,130},{3,131},{4,132},{5,133},{6,134},{7,135},{8... | collective-permute-start | bytes 1425416 | tf_op jit(solution)/shard_map/ppermute | solution.py:79
  7.1 1.3 %collective-permute-start = (bf16[576,512]{1,0:T(8,128)(2,1)}, bf16[576,512]{1,0:T(8,128)(2,1)S(1)}, u32[]{:S(2)}, u32[]{:S(2)}) collective-permute-start(bf16[576,512]{1,0:T(8,128)(2,1)} %get-tuple-element.29), channel_id=1, source_target_pairs={{128,0},{129,1},{130,2},{131,3},{132,4},{133,5},{134,6},{135,7},{1... | collective-permute-start | bytes 1769480 | tf_op jit(solution)/shard_map/ppermute | solution.py:80
  8.9 2.9 %copy.11 = bf16[1,1024,896]{1,2,0:T(8,128)(2,1)S(1)} copy(bf16[1,1024,896]{2,1,0:T(8,128)(2,1)} %param.10) | data formatting | bytes 3670016 | tf_op args[2]
  12.1 1.0 copy-done.9
  13.1 3.0 %fusion.turned_ref = bf16[896,1024]{1,0:T(8,128)(2,1)S(1)} fusion(s32[]{:T(128)S(6)} %select_n.60, bf16[896,1024]{1,0:T(8,128)(2,1)} %bitcast.205), kind=kLoop, calls=%fused_computation.2 | loop fusion | flops 3670016 | bytes 3670020 | tf_op jit(solution)/shard_map/concatenate | solution.py:255
  16.8 1.6 %shard_map.85 = f32[4,448]{1,0:T(4,128)S(1)} custom-call(s32[1,512]{1,0:T(1,128)S(1)} %copy-done.3, bf16[1024,512]{1,0:T(8,128)(2,1)S(1)} %bitcast.202, bf16[464,512]{1,0:T(8,128)(2,1)} %collective-permute-done.1.refs_0_), custom_call_target="tpu_custom_call" | custom-call | tf_op jit(solution)/shard_map/pallas_call | solution.py:69
  18.4 1.4 %collective-permute-start.2 = (f32[4,448]{1,0:T(4,128)S(1)}, f32[4,448]{1,0:T(4,128)S(1)}, u32[]{:S(2)}, u32[]{:S(2)}) collective-permute-start(f32[4,448]{1,0:T(4,128)S(1)} %shard_map.85), channel_id=1, source_target_pairs={{128,0},{129,1},{130,2},{131,3},{132,4},{133,5},{134,6},{135,7},{1... | collective-permute-start | bytes 21512 | tf_op jit(solution)/shard_map/ppermute | solution.py:84
  19.8 4.4 %collective-permute-done.2 = f32[4,448]{1,0:T(4,128)S(1)} collective-permute-done((f32[4,448]{1,0:T(4,128)S(1)}, f32[4,448]{1,0:T(4,128)S(1)}, u32[]{:S(2)}, u32[]{:S(2)}) %collective-permute-start.2) | collective-permute-done | bytes 7200 | tf_op jit(solution)/shard_map/ppermute | solution.py:84
  25.0 1.2 %collective-permute-done.3 = f32[4,1024]{1,0:T(4,128)S(1)} collective-permute-done((f32[4,1024]{1,0:T(4,128)S(1)}, f32[4,1024]{1,0:T(4,128)S(1)}, u32[]{:S(2)}, u32[]{:S(2)}) %collective-permute-start.3) | collective-permute-done | bytes 16416 | tf_op jit(solution)/shard_map/ppermute | solution.py:88
  26.9 7.1 %all-to-all-start = ((f32[8,4,1024]{2,1,0:T(4,128)}), f32[8,4,1024]{2,1,0:T(4,128)S(1)}, u32[]{:S(2)}, u32[]{:S(2)}) async-start(f32[8,4,1024]{2,1,0:T(4,128)} %broadcast_in_dim.117), calls=%async_computation | async-start | bytes 262144 | tf_op jit(solution)/shard_map/all_to_all | solution.py:91
  34.1 6.5 %all-to-all-done = f32[8,4,1024]{2,1,0:T(4,128)S(1)} async-done(((f32[8,4,1024]{2,1,0:T(4,128)}), f32[8,4,1024]{2,1,0:T(4,128)S(1)}, u32[]{:S(2)}, u32[]{:S(2)}) %all-to-all-start) | async-done | bytes 131104 | tf_op jit(solution)/shard_map/all_to_all | solution.py:91
  41.6 2.0 %collective-permute-start.4 = (f16[400,128]{1,0:T(8,128)(2,1)S(1)}, f16[400,128]{1,0:T(8,128)(2,1)S(1)}, u32[]{:S(2)}, u32[]{:S(2)}) collective-permute-start(f16[400,128]{1,0:T(8,128)(2,1)S(1)} %select_convert_fusion.2), channel_id=1, source_target_pairs={{0,16},{16,32},{32,48},{48,64},{64,80},{80,96},{96,112},{112,0},{1... | collective-permute-start | bytes 307208 | tf_op jit(solution)/shard_map/ppermute | solution.py:23
  43.6 3.8 %shard_map.86 = (bf16[4,896,1024]{2,1,0:T(8,128)(2,1)S(1)}, f32[2,1184,128]{2,1,0:T(8,128)S(1)}) custom-call(s32[2,4]{1,0:T(2,128)S(1)} %copy-done.7, f32[4,1024]{1,0:T(4,128)S(1)} %broadcast_multiply_fusion.factors_ref.weight_ref, bf16[896,1024]{1,0:T(8,128)(2,1)S(1)} %fusion.turned_ref), custom_call_target="tpu_custom_call" | custom-call | flops 1 | bytes 1 | tf_op jit(solution)/shard_map/pallas_call | solution.py:188
  47.6 2.0 %collective-permute-start.5 = (f16[1184,128]{1,0:T(8,128)(2,1)S(1)}, f16[1184,128]{1,0:T(8,128)(2,1)S(1)}, u32[]{:S(2)}, u32[]{:S(2)}) collective-permute-start(f16[1184,128]{1,0:T(8,128)(2,1)S(1)} %get-tuple-element.76), channel_id=1, source_target_pairs={{0,16},{16,32},{32,48},{48,64},{64,80},{80,96},{96,112},{112,0},{1... | collective-permute-start | bytes 909320 | tf_op jit(solution)/shard_map/ppermute | solution.py:23
  49.6 2.3 %collective-permute-start.6 = (f16[1184,128]{1,0:T(8,128)(2,1)S(1)}, f16[1184,128]{1,0:T(8,128)(2,1)S(1)}, u32[]{:S(2)}, u32[]{:S(2)}) collective-permute-start(f16[1184,128]{1,0:T(8,128)(2,1)S(1)} %get-tuple-element.75), channel_id=1, source_target_pairs={{0,112},{16,0},{32,16},{48,32},{64,48},{80,64},{96,80},{112,96},{1... | collective-permute-start | bytes 909320 | tf_op jit(solution)/shard_map/ppermute | solution.py:23
  51.9 2.8 %shard_map.88 = f32[2,1184,128]{2,1,0:T(8,128)S(1)} custom-call(s32[2,4]{1,0:T(2,128)S(1)} %copy-done.8, bf16[4,896,1024]{2,1,0:T(8,128)(2,1)S(1)} %get-tuple-element.48.factors_ref, bf16[896,1024]{1,0:T(8,128)(2,1)S(1)} %fusion.turned_ref), custom_call_target="tpu_custom_call" | custom-call | flops 1 | bytes 1 | tf_op jit(solution)/shard_map/pallas_call | solution.py:188
  55.2 3.2 %collective-permute-start.8 = (f16[1184,128]{1,0:T(8,128)(2,1)S(1)}, f16[1184,128]{1,0:T(8,128)(2,1)S(1)}, u32[]{:S(2)}, u32[]{:S(2)}) collective-permute-start(f16[1184,128]{1,0:T(8,128)(2,1)S(1)} %get-tuple-element.77), channel_id=1, source_target_pairs={{0,112},{16,0},{32,16},{48,32},{64,48},{80,64},{96,80},{112,96},{1... | collective-permute-start | bytes 909320 | tf_op jit(solution)/shard_map/ppermute | solution.py:23
  58.4 5.1 %shard_map.89 = f32[4,1184,128]{2,1,0:T(8,128)S(1)} custom-call(s32[4,4]{1,0:T(4,128)S(1)} %copy-done.6, bf16[4,896,1024]{2,1,0:T(8,128)(2,1)S(1)} %get-tuple-element.48.factors_ref, bf16[896,1024]{1,0:T(8,128)(2,1)S(1)} %fusion.turned_ref), custom_call_target="tpu_custom_call" | custom-call | flops 1 | bytes 1 | tf_op jit(solution)/shard_map/pallas_call | solution.py:188
  64.8 1.2 %collective-permute-start.9 = (f16[1184,128]{1,0:T(8,128)(2,1)S(1)}, f16[1184,128]{1,0:T(8,128)(2,1)S(1)}, u32[]{:S(2)}, u32[]{:S(2)}) collective-permute-start(f16[1184,128]{1,0:T(8,128)(2,1)S(1)} %get-tuple-element.68), channel_id=1, source_target_pairs={{0,16},{16,32},{32,48},{48,64},{64,80},{80,96},{96,112},{112,0},{1... | collective-permute-start | bytes 909320 | tf_op jit(solution)/shard_map/ppermute | solution.py:23
  66.4 2.4 %collective-permute-start.13 = (f16[1184,128]{1,0:T(8,128)(2,1)S(1)}, f16[1184,128]{1,0:T(8,128)(2,1)S(1)}, u32[]{:S(2)}, u32[]{:S(2)}) collective-permute-start(f16[1184,128]{1,0:T(8,128)(2,1)S(1)} %get-tuple-element.66), channel_id=1, source_target_pairs={{0,16},{16,32},{32,48},{48,64},{64,80},{80,96},{96,112},{112,0},{1... | collective-permute-start | bytes 909320 | tf_op jit(solution)/shard_map/ppermute | solution.py:23
  69.7 5.1 %shard_map.90 = f32[4,1184,128]{2,1,0:T(8,128)S(1)} custom-call(s32[4,4]{1,0:T(4,128)S(1)} %copy-done.5, bf16[4,896,1024]{2,1,0:T(8,128)(2,1)S(1)} %get-tuple-element.48.factors_ref, bf16[896,1024]{1,0:T(8,128)(2,1)S(1)} %fusion.turned_ref), custom_call_target="tpu_custom_call" | custom-call | flops 1 | bytes 1 | tf_op jit(solution)/shard_map/pallas_call | solution.py:188
  76.6 2.8 %collective-permute-start.12 = (f16[1184,128]{1,0:T(8,128)(2,1)S(1)}, f16[1184,128]{1,0:T(8,128)(2,1)S(1)}, u32[]{:S(2)}, u32[]{:S(2)}) collective-permute-start(f16[1184,128]{1,0:T(8,128)(2,1)S(1)} %get-tuple-element.63), channel_id=1, source_target_pairs={{0,112},{16,0},{32,16},{48,32},{64,48},{80,64},{96,80},{112,96},{1... | collective-permute-start | bytes 909320 | tf_op jit(solution)/shard_map/ppermute | solution.py:23
  79.4 5.1 %shard_map.91 = f32[4,1184,128]{2,1,0:T(8,128)S(1)} custom-call(s32[4,4]{1,0:T(4,128)S(1)} %copy-done.4, bf16[4,896,1024]{2,1,0:T(8,128)(2,1)S(1)} %get-tuple-element.48.factors_ref, bf16[896,1024]{1,0:T(8,128)(2,1)S(1)} %fusion.turned_ref), custom_call_target="tpu_custom_call" | custom-call | flops 1 | bytes 1 | tf_op jit(solution)/shard_map/pallas_call | solution.py:188
  85.0 3.2 %collective-permute-start.17 = (f16[1184,128]{1,0:T(8,128)(2,1)S(1)}, f16[1184,128]{1,0:T(8,128)(2,1)S(1)}, u32[]{:S(2)}, u32[]{:S(2)}) collective-permute-start(f16[1184,128]{1,0:T(8,128)(2,1)S(1)} %get-tuple-element.57), channel_id=1, source_target_pairs={{0,112},{16,0},{32,16},{48,32},{64,48},{80,64},{96,80},{112,96},{1... | collective-permute-start | bytes 909320 | tf_op jit(solution)/shard_map/ppermute | solution.py:23
  88.4 4.6 %collective-permute-done.15 = f16[1184,128]{1,0:T(8,128)(2,1)S(1)} collective-permute-done((f16[1184,128]{1,0:T(8,128)(2,1)S(1)}, f16[1184,128]{1,0:T(8,128)(2,1)S(1)}, u32[]{:S(2)}, u32[]{:S(2)}) %collective-permute-start.15) | collective-permute-done | bytes 303136 | tf_op jit(solution)/shard_map/ppermute | solution.py:23
  93.3 1.5 %fusion.4 = (f16[1584,128]{1,0:T(8,128)(2,1)S(1)}, f16[1584,128]{1,0:T(8,128)(2,1)S(1)}) fusion(f32[392,128]{1,0:T(8,128)S(1)} %slice_add_fusion.4.refs_3_, f32[1176,128]{1,0:T(8,128)S(1)} %get-tuple-element.132, f32[1584]{0:T(1024)S(1)} %pad.10.clone, f32[128]{0:T(128)S(1)} %get-tuple-element.53, f32[128]{0:T(128)S(1)} %bitcast.206, ...), kind=kLoop, calls=%fused_computation.9 | loop fusion | flops 2027520 | bytes 2426608 | tf_op jit(solution)/shard_map/convert_element_type | solution.py:271
  94.9 3.3 %collective-permute-start.18 = (f16[1584,128]{1,0:T(8,128)(2,1)S(1)}, f16[1584,128]{1,0:T(8,128)(2,1)S(1)}, u32[]{:S(2)}, u32[]{:S(2)}) collective-permute-start(f16[1584,128]{1,0:T(8,128)(2,1)S(1)} %get-tuple-element.110), channel_id=1, source_target_pairs={{0,112},{16,0},{32,16},{48,32},{64,48},{80,64},{96,80},{112,96},{1... | collective-permute-start | bytes 1216520 | tf_op jit(solution)/shard_map/ppermute | solution.py:23
  98.4 5.2 %collective-permute-done.18 = f16[1584,128]{1,0:T(8,128)(2,1)S(1)} collective-permute-done((f16[1584,128]{1,0:T(8,128)(2,1)S(1)}, f16[1584,128]{1,0:T(8,128)(2,1)S(1)}, u32[]{:S(2)}, u32[]{:S(2)}) %collective-permute-start.18) | collective-permute-done | bytes 405536 | tf_op jit(solution)/shard_map/ppermute | solution.py:23
  103.7 3.7 %collective-permute-done.16 = f16[1584,128]{1,0:T(8,128)(2,1)S(1)} collective-permute-done((f16[1584,128]{1,0:T(8,128)(2,1)S(1)}, f16[1584,128]{1,0:T(8,128)(2,1)S(1)}, u32[]{:S(2)}, u32[]{:S(2)}) %collective-permute-start.16) | collective-permute-done | bytes 405536 | tf_op jit(solution)/shard_map/ppermute | solution.py:23
  107.5 2.9 %shard_map.92 = f32[112,3584]{1,0:T(8,128)} custom-call(s32[1]{0:T(128)} %bitcast.me_ref, f32[784,128]{1,0:T(8,128)S(1)} %get-tuple-element.74.refs_0_, f32[784,128]{1,0:T(8,128)S(1)} %get-tuple-element.73.refs_1_, f32[392,128]{1,0:T(8,128)S(1)} %slice_add_fusion.5.refs_2_, f32[392,128]{1,0:T(8,128)S(1)} %slice_add_fusion.4.refs_3_, ...), custom_call_target="tpu_custom_call" | custom-call | tf_op jit(solution)/shard_map/pallas_call | solution.py:239
  (82 shorter events, 10.8 us)
Async XLA Ops:
  0.0 1.2 %copy-start = (bf16[1,1024,512]{2,1,0:T(8,128)(2,1)S(1)}, bf16[1,1024,512]{2,1,0:T(8,128)(2,1)}, u32[]{:S(2)}) copy-start(bf16[1,1024,512]{2,1,0:T(8,128)(2,1)} %param.8) | copy-start | bytes 3145732
  1.2 0.7 copy-start.2
  3.0 13.8 %collective-permute-start.1 = (bf16[464,512]{1,0:T(8,128)(2,1)}, bf16[464,512]{1,0:T(8,128)(2,1)}, u32[]{:S(2)}, u32[]{:S(2)}) collective-permute-start(bf16[464,512]{1,0:T(8,128)(2,1)} %get-tuple-element.30), channel_id=1, source_target_pairs={{0,128},{1,129},{2,130},{3,131},{4,132},{5,133},{6,134},{7,135},{8... | collective-permute-start | bytes 1425416 | tf_op jit(solution)/shard_map/ppermute | solution.py:79
  7.1 17.1 %collective-permute-start = (bf16[576,512]{1,0:T(8,128)(2,1)}, bf16[576,512]{1,0:T(8,128)(2,1)S(1)}, u32[]{:S(2)}, u32[]{:S(2)}) collective-permute-start(bf16[576,512]{1,0:T(8,128)(2,1)} %get-tuple-element.29), channel_id=1, source_target_pairs={{128,0},{129,1},{130,2},{131,3},{132,4},{133,5},{134,6},{135,7},{1... | collective-permute-start | bytes 1769480 | tf_op jit(solution)/shard_map/ppermute | solution.py:80
  11.9 1.3 %copy-start.9 = (bf16[1,1024,896]{1,2,0:T(8,128)(2,1)}, bf16[1,1024,896]{1,2,0:T(8,128)(2,1)S(1)}, u32[]{:S(2)}) copy-start(bf16[1,1024,896]{1,2,0:T(8,128)(2,1)S(1)} %copy.11) | copy-start | bytes 5505028
  11.9 4.9 %copy-start.1 = (bf16[1,1024,512]{2,1,0:T(8,128)(2,1)S(1)}, bf16[1,1024,512]{2,1,0:T(8,128)(2,1)}, u32[]{:S(2)}) copy-start(bf16[1,1024,512]{2,1,0:T(8,128)(2,1)} %param.8) | copy-start | bytes 3145732
  11.9 4.9 %copy-start.3 = (s32[1,512]{1,0:T(1,128)S(1)}, s32[1,512]{1,0:T(1,128)}, u32[]{:S(2)}) copy-start(s32[1,512]{1,0:T(1,128)} %groups_ref.7) | copy-start | bytes 6148
  18.3 25.2 %copy-start.7 = (s32[2,4]{1,0:T(2,128)S(1)}, s32[2,4]{1,0:T(2,128)}, u32[]{:S(2)}) copy-start(s32[2,4]{1,0:T(2,128)} %constant.62.clone.table_ref) | copy-start | bytes 100
  18.4 5.8 %collective-permute-start.2 = (f32[4,448]{1,0:T(4,128)S(1)}, f32[4,448]{1,0:T(4,128)S(1)}, u32[]{:S(2)}, u32[]{:S(2)}) collective-permute-start(f32[4,448]{1,0:T(4,128)S(1)} %shard_map.85), channel_id=1, source_target_pairs={{128,0},{129,1},{130,2},{131,3},{132,4},{133,5},{134,6},{135,7},{1... | collective-permute-start | bytes 21512 | tf_op jit(solution)/shard_map/ppermute | solution.py:84
  25.0 1.2 %collective-permute-start.3 = (f32[4,1024]{1,0:T(4,128)S(1)}, f32[4,1024]{1,0:T(4,128)S(1)}, u32[]{:S(2)}, u32[]{:S(2)}) collective-permute-start(f32[4,1024]{1,0:T(4,128)S(1)} %pad_maximum_fusion), channel_id=1, source_target_pairs={{0,1},{1,0},{2,3},{3,2},{4,5},{5,4},{6,7},{7,6},{8,9},{9,8},{10,11... | collective-permute-start | bytes 49160 | tf_op jit(solution)/shard_map/ppermute | solution.py:88
  26.9 13.7 %all-to-all-start = ((f32[8,4,1024]{2,1,0:T(4,128)}), f32[8,4,1024]{2,1,0:T(4,128)S(1)}, u32[]{:S(2)}, u32[]{:S(2)}) async-start(f32[8,4,1024]{2,1,0:T(4,128)} %broadcast_in_dim.117), calls=%async_computation | async-start | bytes 262144 | tf_op jit(solution)/shard_map/all_to_all | solution.py:91
  41.4 10.5 %copy-start.8 = (s32[2,4]{1,0:T(2,128)S(1)}, s32[2,4]{1,0:T(2,128)}, u32[]{:S(2)}) copy-start(s32[2,4]{1,0:T(2,128)} %constant.63.clone.table_ref) | copy-start | bytes 100
  41.6 13.2 %collective-permute-start.4 = (f16[400,128]{1,0:T(8,128)(2,1)S(1)}, f16[400,128]{1,0:T(8,128)(2,1)S(1)}, u32[]{:S(2)}, u32[]{:S(2)}) collective-permute-start(f16[400,128]{1,0:T(8,128)(2,1)S(1)} %select_convert_fusion.2), channel_id=1, source_target_pairs={{0,16},{16,32},{32,48},{48,64},{64,80},{80,96},{96,112},{112,0},{1... | collective-permute-start | bytes 307208 | tf_op jit(solution)/shard_map/ppermute | solution.py:23
  47.6 15.9 %collective-permute-start.5 = (f16[1184,128]{1,0:T(8,128)(2,1)S(1)}, f16[1184,128]{1,0:T(8,128)(2,1)S(1)}, u32[]{:S(2)}, u32[]{:S(2)}) collective-permute-start(f16[1184,128]{1,0:T(8,128)(2,1)S(1)} %get-tuple-element.76), channel_id=1, source_target_pairs={{0,16},{16,32},{32,48},{48,64},{64,80},{80,96},{96,112},{112,0},{1... | collective-permute-start | bytes 909320 | tf_op jit(solution)/shard_map/ppermute | solution.py:23
  49.6 13.9 %collective-permute-start.6 = (f16[1184,128]{1,0:T(8,128)(2,1)S(1)}, f16[1184,128]{1,0:T(8,128)(2,1)S(1)}, u32[]{:S(2)}, u32[]{:S(2)}) collective-permute-start(f16[1184,128]{1,0:T(8,128)(2,1)S(1)} %get-tuple-element.75), channel_id=1, source_target_pairs={{0,112},{16,0},{32,16},{48,32},{64,48},{80,64},{96,80},{112,96},{1... | collective-permute-start | bytes 909320 | tf_op jit(solution)/shard_map/ppermute | solution.py:23
  51.9 6.5 %copy-start.6 = (s32[4,4]{1,0:T(4,128)S(1)}, s32[4,4]{1,0:T(4,128)}, u32[]{:S(2)}) copy-start(s32[4,4]{1,0:T(4,128)} %constant.64.clone.table_ref) | copy-start | bytes 196
  55.1 11.0 %collective-permute-start.7 = (f16[1184,128]{1,0:T(8,128)(2,1)S(1)}, f16[1184,128]{1,0:T(8,128)(2,1)S(1)}, u32[]{:S(2)}, u32[]{:S(2)}) collective-permute-start(f16[1184,128]{1,0:T(8,128)(2,1)S(1)} %get-tuple-element.78), channel_id=1, source_target_pairs={{0,16},{16,32},{32,48},{48,64},{64,80},{80,96},{96,112},{112,0},{1... | collective-permute-start | bytes 909320 | tf_op jit(solution)/shard_map/ppermute | solution.py:23
  55.2 10.9 %collective-permute-start.8 = (f16[1184,128]{1,0:T(8,128)(2,1)S(1)}, f16[1184,128]{1,0:T(8,128)(2,1)S(1)}, u32[]{:S(2)}, u32[]{:S(2)}) collective-permute-start(f16[1184,128]{1,0:T(8,128)(2,1)S(1)} %get-tuple-element.77), channel_id=1, source_target_pairs={{0,112},{16,0},{32,16},{48,32},{64,48},{80,64},{96,80},{112,96},{1... | collective-permute-start | bytes 909320 | tf_op jit(solution)/shard_map/ppermute | solution.py:23
  63.6 6.2 %copy-start.5 = (s32[4,4]{1,0:T(4,128)S(1)}, s32[4,4]{1,0:T(4,128)}, u32[]{:S(2)}) copy-start(s32[4,4]{1,0:T(4,128)} %constant.65.clone.table_ref) | copy-start | bytes 196
  64.0 10.9 %collective-permute-start.10 = (f16[1184,128]{1,0:T(8,128)(2,1)S(1)}, f16[1184,128]{1,0:T(8,128)(2,1)S(1)}, u32[]{:S(2)}, u32[]{:S(2)}) collective-permute-start(f16[1184,128]{1,0:T(8,128)(2,1)S(1)} %get-tuple-element.67), channel_id=1, source_target_pairs={{0,112},{16,0},{32,16},{48,32},{64,48},{80,64},{96,80},{112,96},{1... | collective-permute-start | bytes 909320 | tf_op jit(solution)/shard_map/ppermute | solution.py:23
  64.8 10.9 %collective-permute-start.9 = (f16[1184,128]{1,0:T(8,128)(2,1)S(1)}, f16[1184,128]{1,0:T(8,128)(2,1)S(1)}, u32[]{:S(2)}, u32[]{:S(2)}) collective-permute-start(f16[1184,128]{1,0:T(8,128)(2,1)S(1)} %get-tuple-element.68), channel_id=1, source_target_pairs={{0,16},{16,32},{32,48},{48,64},{64,80},{80,96},{96,112},{112,0},{1... | collective-permute-start | bytes 909320 | tf_op jit(solution)/shard_map/ppermute | solution.py:23
  66.4 18.1 %collective-permute-start.13 = (f16[1184,128]{1,0:T(8,128)(2,1)S(1)}, f16[1184,128]{1,0:T(8,128)(2,1)S(1)}, u32[]{:S(2)}, u32[]{:S(2)}) collective-permute-start(f16[1184,128]{1,0:T(8,128)(2,1)S(1)} %get-tuple-element.66), channel_id=1, source_target_pairs={{0,16},{16,32},{32,48},{48,64},{64,80},{80,96},{96,112},{112,0},{1... | collective-permute-start | bytes 909320 | tf_op jit(solution)/shard_map/ppermute | solution.py:23
  68.9 15.7 %collective-permute-start.14 = (f16[1184,128]{1,0:T(8,128)(2,1)S(1)}, f16[1184,128]{1,0:T(8,128)(2,1)S(1)}, u32[]{:S(2)}, u32[]{:S(2)}) collective-permute-start(f16[1184,128]{1,0:T(8,128)(2,1)S(1)} %get-tuple-element.65), channel_id=1, source_target_pairs={{0,112},{16,0},{32,16},{48,32},{64,48},{80,64},{96,80},{112,96},{1... | collective-permute-start | bytes 909320 | tf_op jit(solution)/shard_map/ppermute | solution.py:23
  74.9 4.5 %copy-start.4 = (s32[4,4]{1,0:T(4,128)S(1)}, s32[4,4]{1,0:T(4,128)}, u32[]{:S(2)}) copy-start(s32[4,4]{1,0:T(4,128)} %constant.66.clone.table_ref) | copy-start | bytes 196
  76.1 12.3 %collective-permute-start.11 = (f16[1184,128]{1,0:T(8,128)(2,1)S(1)}, f16[1184,128]{1,0:T(8,128)(2,1)S(1)}, u32[]{:S(2)}, u32[]{:S(2)}) collective-permute-start(f16[1184,128]{1,0:T(8,128)(2,1)S(1)} %get-tuple-element.64), channel_id=1, source_target_pairs={{0,16},{16,32},{32,48},{48,64},{64,80},{80,96},{96,112},{112,0},{1... | collective-permute-start | bytes 909320 | tf_op jit(solution)/shard_map/ppermute | solution.py:23
  76.6 11.8 %collective-permute-start.12 = (f16[1184,128]{1,0:T(8,128)(2,1)S(1)}, f16[1184,128]{1,0:T(8,128)(2,1)S(1)}, u32[]{:S(2)}, u32[]{:S(2)}) collective-permute-start(f16[1184,128]{1,0:T(8,128)(2,1)S(1)} %get-tuple-element.63), channel_id=1, source_target_pairs={{0,112},{16,0},{32,16},{48,32},{64,48},{80,64},{96,80},{112,96},{1... | collective-permute-start | bytes 909320 | tf_op jit(solution)/shard_map/ppermute | solution.py:23
  84.9 8.1 %collective-permute-start.15 = (f16[1184,128]{1,0:T(8,128)(2,1)S(1)}, f16[1184,128]{1,0:T(8,128)(2,1)S(1)}, u32[]{:S(2)}, u32[]{:S(2)}) collective-permute-start(f16[1184,128]{1,0:T(8,128)(2,1)S(1)} %get-tuple-element.61), channel_id=1, source_target_pairs={{0,16},{16,32},{32,48},{48,64},{64,80},{80,96},{96,112},{112,0},{1... | collective-permute-start | bytes 909320 | tf_op jit(solution)/shard_map/ppermute | solution.py:23
  85.0 8.0 %collective-permute-start.17 = (f16[1184,128]{1,0:T(8,128)(2,1)S(1)}, f16[1184,128]{1,0:T(8,128)(2,1)S(1)}, u32[]{:S(2)}, u32[]{:S(2)}) collective-permute-start(f16[1184,128]{1,0:T(8,128)(2,1)S(1)} %get-tuple-element.57), channel_id=1, source_target_pairs={{0,112},{16,0},{32,16},{48,32},{64,48},{80,64},{96,80},{112,96},{1... | collective-permute-start | bytes 909320 | tf_op jit(solution)/shard_map/ppermute | solution.py:23
  94.9 8.7 %collective-permute-start.18 = (f16[1584,128]{1,0:T(8,128)(2,1)S(1)}, f16[1584,128]{1,0:T(8,128)(2,1)S(1)}, u32[]{:S(2)}, u32[]{:S(2)}) collective-permute-start(f16[1584,128]{1,0:T(8,128)(2,1)S(1)} %get-tuple-element.110), channel_id=1, source_target_pairs={{0,112},{16,0},{32,16},{48,32},{64,48},{80,64},{96,80},{112,96},{1... | collective-permute-start | bytes 1216520 | tf_op jit(solution)/shard_map/ppermute | solution.py:23
  98.2 9.2 %collective-permute-start.16 = (f16[1584,128]{1,0:T(8,128)(2,1)S(1)}, f16[1584,128]{1,0:T(8,128)(2,1)S(1)}, u32[]{:S(2)}, u32[]{:S(2)}) collective-permute-start(f16[1584,128]{1,0:T(8,128)(2,1)S(1)} %get-tuple-element.111), channel_id=1, source_target_pairs={{0,16},{16,32},{32,48},{48,64},{64,80},{80,96},{96,112},{112,0},{1... | collective-permute-start | bytes 1216520 | tf_op jit(solution)/shard_map/ppermute | solution.py:23

commit v2 on v1

--- a/solution.py
+++ b/solution.py
@@ -15,7 +15,7 @@
 SENT = jnp.float16
 VMEM_LIMIT = 8 * 1024 * 1024
 PRODUCT_VMEM_LIMIT = 24 * 1024 * 1024
-KEPT = 576
+KEPT = 608
 
 
 def shift(value, axis, steps):

time: 111 us -> 112 us (level)
    ppermute x1, waiting for transfers between devices: 4.39 us -> 5.75 us  [section_weights(): back = lax.ppermute(back, 'section', [(1, 0)])]
  transfers between devices with their start and end apart: 20 -> 20, of which waited for: 8 -> 7; matrix products, arithmetic and copies ran while one was open for 8% -> 8% of each run, Pallas kernels for 22% -> 22%
where the time goes in v2:
time: 112 us; the launch traced here: 111 us
  starting transfers between devices  39.4 us (35%)
  Pallas kernels  29.5 us (26%)
  waiting for transfers between devices  27.7 us (25%)
  other arithmetic  7.63 us (7%)
  local copies, waits for them, and re-layouts  6.82 us (6%)
    ppermute x15, starting transfers between devices, shift(): lax.ppermute(value, axis, [(i, (i + steps) % count) for i in range(count)])  25.4 us
    pallas_call x5, Pallas kernels, products(): pl.pallas_call(functools.partial(product_kernel, make), in_specs=[pl.Bloc...  22 us
    ppermute x15, waiting for transfers between devices, shift(): lax.ppermute(value, axis, [(i, (i + steps) % count) for i in range(count)])  14.3 us
    all_to_all x1, starting transfers between devices, section_weights(): lax.all_to_all(spread, 'tensor', 0, 0, axis_index_groups=chips, tiled=True)  7.08 us
    all_to_all x1, waiting for transfers between devices, section_weights(): lax.all_to_all(spread, 'tensor', 0, 0, axis_index_groups=chips, tiled=True)  6.48 us
    unnamed x21, local copies, waits for them, and re-layouts  5.89 us
    ppermute x1, waiting for transfers between devices, section_weights(): back = lax.ppermute(back, 'section', [(1, 0)])  5.75 us
    ppermute x1, starting transfers between devices, section_weights(): first = lax.ppermute(moved, 'section', [(0, 1)])  4.16 us
  transfers between devices with their start and end apart: 20, of which 7 were waited for; matrix products, arithmetic and copies ran while one was open for 8% of the time, Pallas kernels for 22%

profile of v2, /device:TPU:8, one launch (start us, length us, event | category | flops | bytes accessed | tf_op | source)
XLA Modules:
  0.0 111.5 jit_solution(5212488151657421072)
XLA Ops:
  0.0 1.2 %copy-done = bf16[1,1024,512]{2,1,0:T(8,128)(2,1)S(1)} copy-done((bf16[1,1024,512]{2,1,0:T(8,128)(2,1)S(1)}, bf16[1,1024,512]{2,1,0:T(8,128)(2,1)}, u32[]{:S(2)}) %copy-start) | copy-done | bytes 1048600
  1.9 1.0 shard_map.82
  2.9 4.2 %collective-permute-start.1 = (bf16[432,512]{1,0:T(8,128)(2,1)}, bf16[432,512]{1,0:T(8,128)(2,1)}, u32[]{:S(2)}, u32[]{:S(2)}) collective-permute-start(bf16[432,512]{1,0:T(8,128)(2,1)} %get-tuple-element.30), channel_id=1, source_target_pairs={{0,128},{1,129},{2,130},{3,131},{4,132},{5,133},{6,134},{7,135},{8... | collective-permute-start | bytes 1327112 | tf_op jit(solution)/shard_map/ppermute | solution.py:79
  7.1 1.3 %collective-permute-start = (bf16[608,512]{1,0:T(8,128)(2,1)}, bf16[608,512]{1,0:T(8,128)(2,1)S(1)}, u32[]{:S(2)}, u32[]{:S(2)}) collective-permute-start(bf16[608,512]{1,0:T(8,128)(2,1)} %get-tuple-element.29), channel_id=1, source_target_pairs={{128,0},{129,1},{130,2},{131,3},{132,4},{133,5},{134,6},{135,7},{1... | collective-permute-start | bytes 1867784 | tf_op jit(solution)/shard_map/ppermute | solution.py:80
  8.9 2.9 %copy.11 = bf16[1,1024,896]{1,2,0:T(8,128)(2,1)S(1)} copy(bf16[1,1024,896]{2,1,0:T(8,128)(2,1)} %param.10) | data formatting | bytes 3670016 | tf_op args[2]
  13.1 3.0 %fusion.turned_ref = bf16[896,1024]{1,0:T(8,128)(2,1)S(1)} fusion(s32[]{:T(128)S(6)} %select_n.60, bf16[896,1024]{1,0:T(8,128)(2,1)} %bitcast.205), kind=kLoop, calls=%fused_computation.2 | loop fusion | flops 3670016 | bytes 3670020 | tf_op jit(solution)/shard_map/concatenate | solution.py:255
  16.1 1.5 %shard_map.85 = f32[4,416]{1,0:T(4,128)S(1)} custom-call(s32[1,512]{1,0:T(1,128)S(1)} %copy-done.3, bf16[1024,512]{1,0:T(8,128)(2,1)S(1)} %bitcast.202, bf16[432,512]{1,0:T(8,128)(2,1)} %collective-permute-done.1.refs_0_), custom_call_target="tpu_custom_call" | custom-call | tf_op jit(solution)/shard_map/pallas_call | solution.py:69
  17.7 1.4 %collective-permute-start.2 = (f32[4,416]{1,0:T(4,128)S(1)}, f32[4,416]{1,0:T(4,128)S(1)}, u32[]{:S(2)}, u32[]{:S(2)}) collective-permute-start(f32[4,416]{1,0:T(4,128)S(1)} %shard_map.85), channel_id=1, source_target_pairs={{128,0},{129,1},{130,2},{131,3},{132,4},{133,5},{134,6},{135,7},{1... | collective-permute-start | bytes 19976 | tf_op jit(solution)/shard_map/ppermute | solution.py:84
  19.1 5.7 %collective-permute-done.2 = f32[4,416]{1,0:T(4,128)S(1)} collective-permute-done((f32[4,416]{1,0:T(4,128)S(1)}, f32[4,416]{1,0:T(4,128)S(1)}, u32[]{:S(2)}, u32[]{:S(2)}) %collective-permute-start.2) | collective-permute-done | bytes 6688 | tf_op jit(solution)/shard_map/ppermute | solution.py:84
  25.7 1.2 %collective-permute-done.3 = f32[4,1024]{1,0:T(4,128)S(1)} collective-permute-done((f32[4,1024]{1,0:T(4,128)S(1)}, f32[4,1024]{1,0:T(4,128)S(1)}, u32[]{:S(2)}, u32[]{:S(2)}) %collective-permute-start.3) | collective-permute-done | bytes 16416 | tf_op jit(solution)/shard_map/ppermute | solution.py:88
  27.7 7.1 %all-to-all-start = ((f32[8,4,1024]{2,1,0:T(4,128)}), f32[8,4,1024]{2,1,0:T(4,128)S(1)}, u32[]{:S(2)}, u32[]{:S(2)}) async-start(f32[8,4,1024]{2,1,0:T(4,128)} %broadcast_in_dim.117), calls=%async_computation | async-start | bytes 262144 | tf_op jit(solution)/shard_map/all_to_all | solution.py:91
  34.8 6.5 %all-to-all-done = f32[8,4,1024]{2,1,0:T(4,128)S(1)} async-done(((f32[8,4,1024]{2,1,0:T(4,128)}), f32[8,4,1024]{2,1,0:T(4,128)S(1)}, u32[]{:S(2)}, u32[]{:S(2)}) %all-to-all-start) | async-done | bytes 131104 | tf_op jit(solution)/shard_map/all_to_all | solution.py:91
  42.3 2.0 %collective-permute-start.4 = (f16[400,128]{1,0:T(8,128)(2,1)S(1)}, f16[400,128]{1,0:T(8,128)(2,1)S(1)}, u32[]{:S(2)}, u32[]{:S(2)}) collective-permute-start(f16[400,128]{1,0:T(8,128)(2,1)S(1)} %select_convert_fusion.2), channel_id=1, source_target_pairs={{0,16},{16,32},{32,48},{48,64},{64,80},{80,96},{96,112},{112,0},{1... | collective-permute-start | bytes 307208 | tf_op jit(solution)/shard_map/ppermute | solution.py:23
  44.3 3.8 %shard_map.86 = (bf16[4,896,1024]{2,1,0:T(8,128)(2,1)S(1)}, f32[2,1184,128]{2,1,0:T(8,128)S(1)}) custom-call(s32[2,4]{1,0:T(2,128)S(1)} %copy-done.7, f32[4,1024]{1,0:T(4,128)S(1)} %broadcast_multiply_fusion.factors_ref.weight_ref, bf16[896,1024]{1,0:T(8,128)(2,1)S(1)} %fusion.turned_ref), custom_call_target="tpu_custom_call" | custom-call | flops 1 | bytes 1 | tf_op jit(solution)/shard_map/pallas_call | solution.py:188
  48.3 2.0 %collective-permute-start.5 = (f16[1184,128]{1,0:T(8,128)(2,1)S(1)}, f16[1184,128]{1,0:T(8,128)(2,1)S(1)}, u32[]{:S(2)}, u32[]{:S(2)}) collective-permute-start(f16[1184,128]{1,0:T(8,128)(2,1)S(1)} %get-tuple-element.76), channel_id=1, source_target_pairs={{0,16},{16,32},{32,48},{48,64},{64,80},{80,96},{96,112},{112,0},{1... | collective-permute-start | bytes 909320 | tf_op jit(solution)/shard_map/ppermute | solution.py:23
  50.3 2.1 %collective-permute-start.6 = (f16[1184,128]{1,0:T(8,128)(2,1)S(1)}, f16[1184,128]{1,0:T(8,128)(2,1)S(1)}, u32[]{:S(2)}, u32[]{:S(2)}) collective-permute-start(f16[1184,128]{1,0:T(8,128)(2,1)S(1)} %get-tuple-element.75), channel_id=1, source_target_pairs={{0,112},{16,0},{32,16},{48,32},{64,48},{80,64},{96,80},{112,96},{1... | collective-permute-start | bytes 909320 | tf_op jit(solution)/shard_map/ppermute | solution.py:23
  52.5 2.8 %shard_map.88 = f32[2,1184,128]{2,1,0:T(8,128)S(1)} custom-call(s32[2,4]{1,0:T(2,128)S(1)} %copy-done.8, bf16[4,896,1024]{2,1,0:T(8,128)(2,1)S(1)} %get-tuple-element.48.factors_ref, bf16[896,1024]{1,0:T(8,128)(2,1)S(1)} %fusion.turned_ref), custom_call_target="tpu_custom_call" | custom-call | flops 1 | bytes 1 | tf_op jit(solution)/shard_map/pallas_call | solution.py:188
  55.9 3.2 %collective-permute-start.8 = (f16[1184,128]{1,0:T(8,128)(2,1)S(1)}, f16[1184,128]{1,0:T(8,128)(2,1)S(1)}, u32[]{:S(2)}, u32[]{:S(2)}) collective-permute-start(f16[1184,128]{1,0:T(8,128)(2,1)S(1)} %get-tuple-element.77), channel_id=1, source_target_pairs={{0,112},{16,0},{32,16},{48,32},{64,48},{80,64},{96,80},{112,96},{1... | collective-permute-start | bytes 909320 | tf_op jit(solution)/shard_map/ppermute | solution.py:23
  59.1 5.1 %shard_map.89 = f32[4,1184,128]{2,1,0:T(8,128)S(1)} custom-call(s32[4,4]{1,0:T(4,128)S(1)} %copy-done.6, bf16[4,896,1024]{2,1,0:T(8,128)(2,1)S(1)} %get-tuple-element.48.factors_ref, bf16[896,1024]{1,0:T(8,128)(2,1)S(1)} %fusion.turned_ref), custom_call_target="tpu_custom_call" | custom-call | flops 1 | bytes 1 | tf_op jit(solution)/shard_map/pallas_call | solution.py:188
  65.5 1.2 %collective-permute-start.9 = (f16[1184,128]{1,0:T(8,128)(2,1)S(1)}, f16[1184,128]{1,0:T(8,128)(2,1)S(1)}, u32[]{:S(2)}, u32[]{:S(2)}) collective-permute-start(f16[1184,128]{1,0:T(8,128)(2,1)S(1)} %get-tuple-element.68), channel_id=1, source_target_pairs={{0,16},{16,32},{32,48},{48,64},{64,80},{80,96},{96,112},{112,0},{1... | collective-permute-start | bytes 909320 | tf_op jit(solution)/shard_map/ppermute | solution.py:23
  67.1 2.3 %collective-permute-start.13 = (f16[1184,128]{1,0:T(8,128)(2,1)S(1)}, f16[1184,128]{1,0:T(8,128)(2,1)S(1)}, u32[]{:S(2)}, u32[]{:S(2)}) collective-permute-start(f16[1184,128]{1,0:T(8,128)(2,1)S(1)} %get-tuple-element.66), channel_id=1, source_target_pairs={{0,16},{16,32},{32,48},{48,64},{64,80},{80,96},{96,112},{112,0},{1... | collective-permute-start | bytes 909320 | tf_op jit(solution)/shard_map/ppermute | solution.py:23
  69.4 1.1 collective-permute-start.14
  70.5 5.1 %shard_map.90 = f32[4,1184,128]{2,1,0:T(8,128)S(1)} custom-call(s32[4,4]{1,0:T(4,128)S(1)} %copy-done.5, bf16[4,896,1024]{2,1,0:T(8,128)(2,1)S(1)} %get-tuple-element.48.factors_ref, bf16[896,1024]{1,0:T(8,128)(2,1)S(1)} %fusion.turned_ref), custom_call_target="tpu_custom_call" | custom-call | flops 1 | bytes 1 | tf_op jit(solution)/shard_map/pallas_call | solution.py:188
  77.3 2.8 %collective-permute-start.12 = (f16[1184,128]{1,0:T(8,128)(2,1)S(1)}, f16[1184,128]{1,0:T(8,128)(2,1)S(1)}, u32[]{:S(2)}, u32[]{:S(2)}) collective-permute-start(f16[1184,128]{1,0:T(8,128)(2,1)S(1)} %get-tuple-element.63), channel_id=1, source_target_pairs={{0,112},{16,0},{32,16},{48,32},{64,48},{80,64},{96,80},{112,96},{1... | collective-permute-start | bytes 909320 | tf_op jit(solution)/shard_map/ppermute | solution.py:23
  80.1 5.1 %shard_map.91 = f32[4,1184,128]{2,1,0:T(8,128)S(1)} custom-call(s32[4,4]{1,0:T(4,128)S(1)} %copy-done.4, bf16[4,896,1024]{2,1,0:T(8,128)(2,1)S(1)} %get-tuple-element.48.factors_ref, bf16[896,1024]{1,0:T(8,128)(2,1)S(1)} %fusion.turned_ref), custom_call_target="tpu_custom_call" | custom-call | flops 1 | bytes 1 | tf_op jit(solution)/shard_map/pallas_call | solution.py:188
  85.9 3.2 %collective-permute-start.17 = (f16[1184,128]{1,0:T(8,128)(2,1)S(1)}, f16[1184,128]{1,0:T(8,128)(2,1)S(1)}, u32[]{:S(2)}, u32[]{:S(2)}) collective-permute-start(f16[1184,128]{1,0:T(8,128)(2,1)S(1)} %get-tuple-element.57), channel_id=1, source_target_pairs={{0,112},{16,0},{32,16},{48,32},{64,48},{80,64},{96,80},{112,96},{1... | collective-permute-start | bytes 909320 | tf_op jit(solution)/shard_map/ppermute | solution.py:23
  89.3 4.6 %collective-permute-done.15 = f16[1184,128]{1,0:T(8,128)(2,1)S(1)} collective-permute-done((f16[1184,128]{1,0:T(8,128)(2,1)S(1)}, f16[1184,128]{1,0:T(8,128)(2,1)S(1)}, u32[]{:S(2)}, u32[]{:S(2)}) %collective-permute-start.15) | collective-permute-done | bytes 303136 | tf_op jit(solution)/shard_map/ppermute | solution.py:23
  94.3 1.5 %fusion.4 = (f16[1584,128]{1,0:T(8,128)(2,1)S(1)}, f16[1584,128]{1,0:T(8,128)(2,1)S(1)}) fusion(f32[392,128]{1,0:T(8,128)S(1)} %slice_add_fusion.4.refs_3_, f32[1176,128]{1,0:T(8,128)S(1)} %get-tuple-element.132, f32[1584]{0:T(1024)S(1)} %pad.10.clone, f32[128]{0:T(128)S(1)} %get-tuple-element.53, f32[128]{0:T(128)S(1)} %bitcast.206, ...), kind=kLoop, calls=%fused_computation.9 | loop fusion | flops 2027520 | bytes 2426608 | tf_op jit(solution)/shard_map/convert_element_type | solution.py:271
  95.8 3.5 %collective-permute-start.18 = (f16[1584,128]{1,0:T(8,128)(2,1)S(1)}, f16[1584,128]{1,0:T(8,128)(2,1)S(1)}, u32[]{:S(2)}, u32[]{:S(2)}) collective-permute-start(f16[1584,128]{1,0:T(8,128)(2,1)S(1)} %get-tuple-element.110), channel_id=1, source_target_pairs={{0,112},{16,0},{32,16},{48,32},{64,48},{80,64},{96,80},{112,96},{1... | collective-permute-start | bytes 1216520 | tf_op jit(solution)/shard_map/ppermute | solution.py:23
  99.5 5.2 %collective-permute-done.18 = f16[1584,128]{1,0:T(8,128)(2,1)S(1)} collective-permute-done((f16[1584,128]{1,0:T(8,128)(2,1)S(1)}, f16[1584,128]{1,0:T(8,128)(2,1)S(1)}, u32[]{:S(2)}, u32[]{:S(2)}) %collective-permute-start.18) | collective-permute-done | bytes 405536 | tf_op jit(solution)/shard_map/ppermute | solution.py:23
  104.8 3.7 %collective-permute-done.16 = f16[1584,128]{1,0:T(8,128)(2,1)S(1)} collective-permute-done((f16[1584,128]{1,0:T(8,128)(2,1)S(1)}, f16[1584,128]{1,0:T(8,128)(2,1)S(1)}, u32[]{:S(2)}, u32[]{:S(2)}) %collective-permute-start.16) | collective-permute-done | bytes 405536 | tf_op jit(solution)/shard_map/ppermute | solution.py:23
  108.6 2.9 %shard_map.92 = f32[112,3584]{1,0:T(8,128)} custom-call(s32[1]{0:T(128)} %bitcast.me_ref, f32[784,128]{1,0:T(8,128)S(1)} %get-tuple-element.74.refs_0_, f32[784,128]{1,0:T(8,128)S(1)} %get-tuple-element.73.refs_1_, f32[392,128]{1,0:T(8,128)S(1)} %slice_add_fusion.5.refs_2_, f32[392,128]{1,0:T(8,128)S(1)} %slice_add_fusion.4.refs_3_, ...), custom_call_target="tpu_custom_call" | custom-call | tf_op jit(solution)/shard_map/pallas_call | solution.py:239
  (82 shorter events, 10.7 us)
Async XLA Ops:
  0.0 1.2 %copy-start = (bf16[1,1024,512]{2,1,0:T(8,128)(2,1)S(1)}, bf16[1,1024,512]{2,1,0:T(8,128)(2,1)}, u32[]{:S(2)}) copy-start(bf16[1,1024,512]{2,1,0:T(8,128)(2,1)} %param.8) | copy-start | bytes 3145732
  1.2 0.7 copy-start.2
  2.9 13.2 %collective-permute-start.1 = (bf16[432,512]{1,0:T(8,128)(2,1)}, bf16[432,512]{1,0:T(8,128)(2,1)}, u32[]{:S(2)}, u32[]{:S(2)}) collective-permute-start(bf16[432,512]{1,0:T(8,128)(2,1)} %get-tuple-element.30), channel_id=1, source_target_pairs={{0,128},{1,129},{2,130},{3,131},{4,132},{5,133},{6,134},{7,135},{8... | collective-permute-start | bytes 1327112 | tf_op jit(solution)/shard_map/ppermute | solution.py:79
  7.1 17.8 %collective-permute-start = (bf16[608,512]{1,0:T(8,128)(2,1)}, bf16[608,512]{1,0:T(8,128)(2,1)S(1)}, u32[]{:S(2)}, u32[]{:S(2)}) collective-permute-start(bf16[608,512]{1,0:T(8,128)(2,1)} %get-tuple-element.29), channel_id=1, source_target_pairs={{128,0},{129,1},{130,2},{131,3},{132,4},{133,5},{134,6},{135,7},{1... | collective-permute-start | bytes 1867784 | tf_op jit(solution)/shard_map/ppermute | solution.py:80
  11.8 1.3 %copy-start.9 = (bf16[1,1024,896]{1,2,0:T(8,128)(2,1)}, bf16[1,1024,896]{1,2,0:T(8,128)(2,1)S(1)}, u32[]{:S(2)}) copy-start(bf16[1,1024,896]{1,2,0:T(8,128)(2,1)S(1)} %copy.11) | copy-start | bytes 5505028
  11.8 4.3 %copy-start.1 = (bf16[1,1024,512]{2,1,0:T(8,128)(2,1)S(1)}, bf16[1,1024,512]{2,1,0:T(8,128)(2,1)}, u32[]{:S(2)}) copy-start(bf16[1,1024,512]{2,1,0:T(8,128)(2,1)} %param.8) | copy-start | bytes 3145732
  11.8 4.3 %copy-start.3 = (s32[1,512]{1,0:T(1,128)S(1)}, s32[1,512]{1,0:T(1,128)}, u32[]{:S(2)}) copy-start(s32[1,512]{1,0:T(1,128)} %groups_ref.7) | copy-start | bytes 6148
  17.7 26.6 %copy-start.7 = (s32[2,4]{1,0:T(2,128)S(1)}, s32[2,4]{1,0:T(2,128)}, u32[]{:S(2)}) copy-start(s32[2,4]{1,0:T(2,128)} %constant.62.clone.table_ref) | copy-start | bytes 100
  17.7 7.2 %collective-permute-start.2 = (f32[4,416]{1,0:T(4,128)S(1)}, f32[4,416]{1,0:T(4,128)S(1)}, u32[]{:S(2)}, u32[]{:S(2)}) collective-permute-start(f32[4,416]{1,0:T(4,128)S(1)} %shard_map.85), channel_id=1, source_target_pairs={{128,0},{129,1},{130,2},{131,3},{132,4},{133,5},{134,6},{135,7},{1... | collective-permute-start | bytes 19976 | tf_op jit(solution)/shard_map/ppermute | solution.py:84
  25.7 1.2 %collective-permute-start.3 = (f32[4,1024]{1,0:T(4,128)S(1)}, f32[4,1024]{1,0:T(4,128)S(1)}, u32[]{:S(2)}, u32[]{:S(2)}) collective-permute-start(f32[4,1024]{1,0:T(4,128)S(1)} %pad_maximum_fusion), channel_id=1, source_target_pairs={{0,1},{1,0},{2,3},{3,2},{4,5},{5,4},{6,7},{7,6},{8,9},{9,8},{10,11... | collective-permute-start | bytes 49160 | tf_op jit(solution)/shard_map/ppermute | solution.py:88
  27.7 13.7 %all-to-all-start = ((f32[8,4,1024]{2,1,0:T(4,128)}), f32[8,4,1024]{2,1,0:T(4,128)S(1)}, u32[]{:S(2)}, u32[]{:S(2)}) async-start(f32[8,4,1024]{2,1,0:T(4,128)} %broadcast_in_dim.117), calls=%async_computation | async-start | bytes 262144 | tf_op jit(solution)/shard_map/all_to_all | solution.py:91
  42.1 10.3 %copy-start.8 = (s32[2,4]{1,0:T(2,128)S(1)}, s32[2,4]{1,0:T(2,128)}, u32[]{:S(2)}) copy-start(s32[2,4]{1,0:T(2,128)} %constant.63.clone.table_ref) | copy-start | bytes 100
  42.3 13.0 %collective-permute-start.4 = (f16[400,128]{1,0:T(8,128)(2,1)S(1)}, f16[400,128]{1,0:T(8,128)(2,1)S(1)}, u32[]{:S(2)}, u32[]{:S(2)}) collective-permute-start(f16[400,128]{1,0:T(8,128)(2,1)S(1)} %select_convert_fusion.2), channel_id=1, source_target_pairs={{0,16},{16,32},{32,48},{48,64},{64,80},{80,96},{96,112},{112,0},{1... | collective-permute-start | bytes 307208 | tf_op jit(solution)/shard_map/ppermute | solution.py:23
  48.3 15.9 %collective-permute-start.5 = (f16[1184,128]{1,0:T(8,128)(2,1)S(1)}, f16[1184,128]{1,0:T(8,128)(2,1)S(1)}, u32[]{:S(2)}, u32[]{:S(2)}) collective-permute-start(f16[1184,128]{1,0:T(8,128)(2,1)S(1)} %get-tuple-element.76), channel_id=1, source_target_pairs={{0,16},{16,32},{32,48},{48,64},{64,80},{80,96},{96,112},{112,0},{1... | collective-permute-start | bytes 909320 | tf_op jit(solution)/shard_map/ppermute | solution.py:23
  50.3 13.9 %collective-permute-start.6 = (f16[1184,128]{1,0:T(8,128)(2,1)S(1)}, f16[1184,128]{1,0:T(8,128)(2,1)S(1)}, u32[]{:S(2)}, u32[]{:S(2)}) collective-permute-start(f16[1184,128]{1,0:T(8,128)(2,1)S(1)} %get-tuple-element.75), channel_id=1, source_target_pairs={{0,112},{16,0},{32,16},{48,32},{64,48},{80,64},{96,80},{112,96},{1... | collective-permute-start | bytes 909320 | tf_op jit(solution)/shard_map/ppermute | solution.py:23
  52.5 6.6 %copy-start.6 = (s32[4,4]{1,0:T(4,128)S(1)}, s32[4,4]{1,0:T(4,128)}, u32[]{:S(2)}) copy-start(s32[4,4]{1,0:T(4,128)} %constant.64.clone.table_ref) | copy-start | bytes 196
  55.6 11.1 %collective-permute-start.7 = (f16[1184,128]{1,0:T(8,128)(2,1)S(1)}, f16[1184,128]{1,0:T(8,128)(2,1)S(1)}, u32[]{:S(2)}, u32[]{:S(2)}) collective-permute-start(f16[1184,128]{1,0:T(8,128)(2,1)S(1)} %get-tuple-element.78), channel_id=1, source_target_pairs={{0,16},{16,32},{32,48},{48,64},{64,80},{80,96},{96,112},{112,0},{1... | collective-permute-start | bytes 909320 | tf_op jit(solution)/shard_map/ppermute | solution.py:23
  55.9 10.9 %collective-permute-start.8 = (f16[1184,128]{1,0:T(8,128)(2,1)S(1)}, f16[1184,128]{1,0:T(8,128)(2,1)S(1)}, u32[]{:S(2)}, u32[]{:S(2)}) collective-permute-start(f16[1184,128]{1,0:T(8,128)(2,1)S(1)} %get-tuple-element.77), channel_id=1, source_target_pairs={{0,112},{16,0},{32,16},{48,32},{64,48},{80,64},{96,80},{112,96},{1... | collective-permute-start | bytes 909320 | tf_op jit(solution)/shard_map/ppermute | solution.py:23
  64.3 6.2 %copy-start.5 = (s32[4,4]{1,0:T(4,128)S(1)}, s32[4,4]{1,0:T(4,128)}, u32[]{:S(2)}) copy-start(s32[4,4]{1,0:T(4,128)} %constant.65.clone.table_ref) | copy-start | bytes 196
  64.7 10.9 %collective-permute-start.10 = (f16[1184,128]{1,0:T(8,128)(2,1)S(1)}, f16[1184,128]{1,0:T(8,128)(2,1)S(1)}, u32[]{:S(2)}, u32[]{:S(2)}) collective-permute-start(f16[1184,128]{1,0:T(8,128)(2,1)S(1)} %get-tuple-element.67), channel_id=1, source_target_pairs={{0,112},{16,0},{32,16},{48,32},{64,48},{80,64},{96,80},{112,96},{1... | collective-permute-start | bytes 909320 | tf_op jit(solution)/shard_map/ppermute | solution.py:23
  65.5 10.9 %collective-permute-start.9 = (f16[1184,128]{1,0:T(8,128)(2,1)S(1)}, f16[1184,128]{1,0:T(8,128)(2,1)S(1)}, u32[]{:S(2)}, u32[]{:S(2)}) collective-permute-start(f16[1184,128]{1,0:T(8,128)(2,1)S(1)} %get-tuple-element.68), channel_id=1, source_target_pairs={{0,16},{16,32},{32,48},{48,64},{64,80},{80,96},{96,112},{112,0},{1... | collective-permute-start | bytes 909320 | tf_op jit(solution)/shard_map/ppermute | solution.py:23
  67.1 18.1 %collective-permute-start.13 = (f16[1184,128]{1,0:T(8,128)(2,1)S(1)}, f16[1184,128]{1,0:T(8,128)(2,1)S(1)}, u32[]{:S(2)}, u32[]{:S(2)}) collective-permute-start(f16[1184,128]{1,0:T(8,128)(2,1)S(1)} %get-tuple-element.66), channel_id=1, source_target_pairs={{0,16},{16,32},{32,48},{48,64},{64,80},{80,96},{96,112},{112,0},{1... | collective-permute-start | bytes 909320 | tf_op jit(solution)/shard_map/ppermute | solution.py:23
  69.4 15.8 %collective-permute-start.14 = (f16[1184,128]{1,0:T(8,128)(2,1)S(1)}, f16[1184,128]{1,0:T(8,128)(2,1)S(1)}, u32[]{:S(2)}, u32[]{:S(2)}) collective-permute-start(f16[1184,128]{1,0:T(8,128)(2,1)S(1)} %get-tuple-element.65), channel_id=1, source_target_pairs={{0,112},{16,0},{32,16},{48,32},{64,48},{80,64},{96,80},{112,96},{1... | collective-permute-start | bytes 909320 | tf_op jit(solution)/shard_map/ppermute | solution.py:23
  75.6 4.5 %copy-start.4 = (s32[4,4]{1,0:T(4,128)S(1)}, s32[4,4]{1,0:T(4,128)}, u32[]{:S(2)}) copy-start(s32[4,4]{1,0:T(4,128)} %constant.66.clone.table_ref) | copy-start | bytes 196
  76.8 12.5 %collective-permute-start.11 = (f16[1184,128]{1,0:T(8,128)(2,1)S(1)}, f16[1184,128]{1,0:T(8,128)(2,1)S(1)}, u32[]{:S(2)}, u32[]{:S(2)}) collective-permute-start(f16[1184,128]{1,0:T(8,128)(2,1)S(1)} %get-tuple-element.64), channel_id=1, source_target_pairs={{0,16},{16,32},{32,48},{48,64},{64,80},{80,96},{96,112},{112,0},{1... | collective-permute-start | bytes 909320 | tf_op jit(solution)/shard_map/ppermute | solution.py:23
  77.3 12.0 %collective-permute-start.12 = (f16[1184,128]{1,0:T(8,128)(2,1)S(1)}, f16[1184,128]{1,0:T(8,128)(2,1)S(1)}, u32[]{:S(2)}, u32[]{:S(2)}) collective-permute-start(f16[1184,128]{1,0:T(8,128)(2,1)S(1)} %get-tuple-element.63), channel_id=1, source_target_pairs={{0,112},{16,0},{32,16},{48,32},{64,48},{80,64},{96,80},{112,96},{1... | collective-permute-start | bytes 909320 | tf_op jit(solution)/shard_map/ppermute | solution.py:23
  85.6 8.3 %collective-permute-start.15 = (f16[1184,128]{1,0:T(8,128)(2,1)S(1)}, f16[1184,128]{1,0:T(8,128)(2,1)S(1)}, u32[]{:S(2)}, u32[]{:S(2)}) collective-permute-start(f16[1184,128]{1,0:T(8,128)(2,1)S(1)} %get-tuple-element.61), channel_id=1, source_target_pairs={{0,16},{16,32},{32,48},{48,64},{64,80},{80,96},{96,112},{112,0},{1... | collective-permute-start | bytes 909320 | tf_op jit(solution)/shard_map/ppermute | solution.py:23
  85.9 8.0 %collective-permute-start.17 = (f16[1184,128]{1,0:T(8,128)(2,1)S(1)}, f16[1184,128]{1,0:T(8,128)(2,1)S(1)}, u32[]{:S(2)}, u32[]{:S(2)}) collective-permute-start(f16[1184,128]{1,0:T(8,128)(2,1)S(1)} %get-tuple-element.57), channel_id=1, source_target_pairs={{0,112},{16,0},{32,16},{48,32},{64,48},{80,64},{96,80},{112,96},{1... | collective-permute-start | bytes 909320 | tf_op jit(solution)/shard_map/ppermute | solution.py:23
  95.8 8.9 %collective-permute-start.18 = (f16[1584,128]{1,0:T(8,128)(2,1)S(1)}, f16[1584,128]{1,0:T(8,128)(2,1)S(1)}, u32[]{:S(2)}, u32[]{:S(2)}) collective-permute-start(f16[1584,128]{1,0:T(8,128)(2,1)S(1)} %get-tuple-element.110), channel_id=1, source_target_pairs={{0,112},{16,0},{32,16},{48,32},{64,48},{80,64},{96,80},{112,96},{1... | collective-permute-start | bytes 1216520 | tf_op jit(solution)/shard_map/ppermute | solution.py:23
  99.3 9.2 %collective-permute-start.16 = (f16[1584,128]{1,0:T(8,128)(2,1)S(1)}, f16[1584,128]{1,0:T(8,128)(2,1)S(1)}, u32[]{:S(2)}, u32[]{:S(2)}) collective-permute-start(f16[1584,128]{1,0:T(8,128)(2,1)S(1)} %get-tuple-element.111), channel_id=1, source_target_pairs={{0,16},{16,32},{32,48},{48,64},{64,80},{80,96},{96,112},{112,0},{1... | collective-permute-start | bytes 1216520 | tf_op jit(solution)/shard_map/ppermute | solution.py:23
